TPU v7x, 32 devices: a whole 2x2x4 slice. The times are simulated.
32 devices in a mesh: chan: 8 (over z, core), tm: 4 (over y, x).
Axes of the slice: x: 2, y: 2, z: 4, core: 2. Of those that a mesh axis runs over, the one named last changes fastest.
Arguments:
- traces: float32 [256, 65536], P('chan', 'tm'), may hold values from -8 to 8
- live_channel: int32 [256], P('chan'), may hold values 0 or 1
- valid_segment: int32 [256, 256], P('chan', 'tm'), may hold values 0 or 1
Outputs:
- correlation: float32 [256, 256, 256], P('chan', 'tm')
All inputs are finite; a program needn't handle non-finite values. No bound on the sum of `live_channel` or of `valid_segment` on one device may be relied on, other than what follows from the above.
Results may differ from a plain program's by a relative error of at most 0.003.
Values may be sent and summed in bfloat16 or wider, within the bound.
A program may use at most 192 MiB of HBM per device.

v0:
```python
import jax
import jax.numpy as jnp
from jax import lax
from jax.sharding import PartitionSpec as P

SEG_LEN = 256
BINS = 128
HALF_WIN = 64
SMOOTH = 4


def with_halo(array, sides, width):
    for axis, dim in sides:
        count, length = (lax.axis_size(axis), array.shape[dim])
        up = [(i, (i + 1) % count) for i in range(count - 1)]
        down = [(j, i) for i, j in up]
        last = lax.slice_in_dim(array, length - width, length, axis=dim)
        first = lax.slice_in_dim(array, 0, width, axis=dim)
        before = lax.ppermute(last, axis, up)
        after = lax.ppermute(first, axis, down)
        array = jnp.concatenate([before, array, after], axis=dim)
    return array


def make_tables():
    length = SEG_LEN
    times_col = jnp.arange(length, dtype=jnp.int32)[:, None]
    freq_row = jnp.arange(BINS, dtype=jnp.int32)[None, :]
    phase = 2.0 * jnp.pi / length * (times_col * freq_row % length).astype(jnp.float32)
    forward_table = jnp.concatenate([jnp.cos(phase), -jnp.sin(phase)], axis=1)
    freq_col = jnp.arange(BINS, dtype=jnp.int32)[:, None]
    lag_row = jnp.arange(length, dtype=jnp.int32)[None, :] - BINS
    back_phase = 2.0 * jnp.pi / length * (freq_col * lag_row % length).astype(jnp.float32)
    inverse_table = jnp.concatenate([jnp.cos(back_phase), -jnp.sin(back_phase)], axis=0)
    bin_a = jnp.arange(BINS, dtype=jnp.int32)[:, None]
    bin_b = jnp.arange(BINS, dtype=jnp.int32)[None, :]
    smooth_table = (jnp.abs(bin_a - bin_b) <= SMOOTH).astype(jnp.float32) / (2.0 * SMOOTH + 1.0)
    bandpass = (jnp.arange(BINS, dtype=jnp.int32) > 0).astype(jnp.float32)
    sample_in = jnp.arange(SEG_LEN + 2 * HALF_WIN, dtype=jnp.int32)[:, None]
    sample_out = jnp.arange(SEG_LEN, dtype=jnp.int32)[None, :]
    inside = (sample_in >= sample_out) & (sample_in <= sample_out + 2 * HALF_WIN)
    box_table = inside.astype(jnp.float32) / (2.0 * HALF_WIN + 1.0)
    return (forward_table, inverse_table, smooth_table, bandpass, box_table)


def make_accumulate(local_spec, local_mask, pieces):
    spec_block, mask_block = pieces
    turned = jnp.stack([spec_block[:, :, 1], -spec_block[:, :, 0]], axis=2)
    cross_real = jnp.einsum(
        "iscf,jscf->ijf", local_spec, spec_block, preferred_element_type=jnp.float32
    )
    cross_imag = jnp.einsum(
        "iscf,jscf->ijf", local_spec, turned, preferred_element_type=jnp.float32
    )
    block_cross = jnp.stack([cross_real, cross_imag], axis=2)
    block_count = jnp.dot(local_mask, mask_block.T, preferred_element_type=jnp.float32)
    return (block_cross, block_count)


def body(traces, live_channel, valid_segment):
    forward_table, inverse_table, smooth_table, bandpass, box_table = make_tables()
    highest = lax.Precision.HIGHEST
    chan_rows = traces.shape[0]
    seg_count = valid_segment.shape[1]
    span = seg_count * SEG_LEN
    magnitude = jnp.abs(traces)
    slab_ends = jnp.concatenate([magnitude[:, :HALF_WIN], magnitude[:, span - HALF_WIN :]], axis=1)
    rims = with_halo(slab_ends, (("tm", 1),), HALF_WIN)
    padded = jnp.concatenate(
        [rims[:, :HALF_WIN], magnitude, rims[:, rims.shape[1] - HALF_WIN :]], axis=1
    )
    head_part = padded[:, :span].reshape(chan_rows, seg_count, SEG_LEN)
    extended = jnp.pad(padded, ((0, 0), (0, SEG_LEN - 2 * HALF_WIN)))
    tail_part = extended[:, SEG_LEN : SEG_LEN + span].reshape(chan_rows, seg_count, SEG_LEN)[
        :, :, : 2 * HALF_WIN
    ]
    window = jnp.concatenate([head_part, tail_part], axis=2)
    abs_level = jnp.dot(window, box_table, precision=highest, preferred_element_type=jnp.float32)
    normed = traces.reshape(chan_rows, seg_count, SEG_LEN) / (abs_level + 1e-05)
    spectrum = jnp.dot(normed, forward_table, precision=highest, preferred_element_type=jnp.float32)
    spectrum = spectrum.reshape(chan_rows, seg_count, 2, BINS)
    spectral_power = spectrum[:, :, 0] ** 2 + spectrum[:, :, 1] ** 2
    smoothed = jnp.dot(
        spectral_power, smooth_table, precision=highest, preferred_element_type=jnp.float32
    )
    mean_power = jnp.mean(spectral_power, axis=-1, keepdims=True)
    seg_mask = (live_channel[:, None] * valid_segment).astype(jnp.bfloat16)
    whiten_scale = (
        bandpass
        * seg_mask.astype(jnp.float32)[:, :, None]
        / jnp.sqrt(smoothed + 0.1 * mean_power + 1e-06)
    )
    whitened = (spectrum * whiten_scale[:, :, None, :]).astype(jnp.bfloat16)
    cross_all, count_all = make_accumulate(
        whitened,
        seg_mask,
        (
            lax.all_gather(whitened, "chan", axis=0, tiled=True),
            lax.all_gather(seg_mask, "chan", axis=0, tiled=True),
        ),
    )
    cross_mine, count_mine = (
        lax.psum_scatter(cross_all, "tm", scatter_dimension=1, tiled=True),
        lax.psum_scatter(count_all, "tm", scatter_dimension=1, tiled=True),
    )
    col_count = cross_mine.shape[1]
    flat_cross = cross_mine.reshape(chan_rows, col_count, 2 * BINS)
    lagged = jnp.dot(
        flat_cross, inverse_table, precision=highest, preferred_element_type=jnp.float32
    )
    return lagged * (2.0 / jnp.maximum(count_mine, 1.0))[:, :, None]


def solution(mesh):
    return jax.shard_map(
        body,
        mesh=mesh,
        in_specs=(P("chan", "tm"), P("chan"), P("chan", "tm")),
        out_specs=P("chan", "tm", None),
        check_vma=False,
    )
```

profile of v0, /device:TPU:1, one launch (start us, length us, event | category | flops | bytes accessed | tf_op | source)
XLA Modules:
  0.0 344.4 jit_solution(10570938235013922364)
XLA Ops:
  7.4 0.0 all-gather.2.cloned.1.call-start
  7.4 1.9 abs.6
  9.3 0.1 fusion.61
  9.4 3.9 %collective-permute-start = (f32[32,64]{1,0:T(8,128)S(1)}, f32[32,64]{1,0:T(8,128)S(1)}, u32[]{:S(2)}, u32[]{:S(2)}) collective-permute-start(f32[32,64]{1,0:T(8,128)S(1)} %get-tuple-element.12), channel_id=1, source_target_pairs={{0,1},{1,2},{2,3},{4,5},{5,6},{6,7},{8,9},{9,10},{10,11},{12,13},{... | collective-permute-start | bytes 24584 | tf_op jit(solution)/shard_map/ppermute | solution.py:19
  13.3 1.3 collective-permute-start.1
  14.6 0.5 sine_negate_fusion.1
  15.2 0.1 fusion.58
  15.3 0.0 copy-done.1
  15.3 2.0 copy.30
  17.2 0.0 collective-permute-done
  17.2 0.6 collective-permute-done.1
  17.8 2.4 concatenate.16
  20.2 1.7 pad_slice_fusion
  21.9 0.6 copy.32
  22.6 0.1 slice.39
  22.6 0.6 pad_maximum_fusion.1
  23.3 0.6 copy.31
  23.9 0.9 copy-done.2
  24.8 3.9 %bitcast_divide_fusion = f32[32,64,256]{2,1,0:T(8,128)S(1)} fusion(f32[4,8,64,256]{3,2,1,0:T(8,128)S(1)} %copy-done.2, f32[32,64,128]{2,1,0:T(8,128)S(1)} %slice.39, f32[32,64,256]{2,1,0:T(8,128)S(1)} %bitcast.56, s32[256]{0:T(256)S(1)} %iota_add_fusion.1), kind=kOutput, calls=%fused_computation.14 | convolution fusion | flops 2418147328 | bytes 7341056 | tf_op jit(solution)/shard_map/dot_general | solution.py:78
  28.8 3.1 fusion.22
  31.9 2.3 reshape.44
  34.2 3.5 %copy.19 = f32[32,64,2,128]{1,0,2,3:T(8,128)} copy(f32[32,64,2,128]{3,2,1,0:T(2,128)S(1)} %reshape.44) | data formatting | bytes 4194304 | tf_op jit(solution)/shard_map/reshape | solution.py:81
  37.7 2.3 fusion.60
  40.0 0.4 fusion.21
  40.4 1.0 fusion.15
  41.4 1.8 copy.18
  43.3 4.6 %multiply_convert_fusion = bf16[32,64,2,128]{1,0,2,3:T(8,128)(2,1)} fusion(f32[32,64,2,128]{1,0,2,3:T(8,128)} %copy.19, f32[32,64,128]{1,0,2:T(8,128)S(1)} %copy.18), kind=kLoop, calls=%fused_computation.6 | loop fusion | flops 1048576 | bytes 4194304 | tf_op jit(solution)/shard_map/convert_element_type | solution.py:93
  47.8 0.0 all-gather.2.cloned.1.call-update
  47.8 0.0 reduce-scatter.7.cloned.1.call-start
  47.9 16.1 %all_gather.7 = bf16[256,64]{1,0:T(8,128)(2,1)S(1)} all-gather(bf16[32,64]{1,0:T(8,128)(2,1)S(1)} %get-tuple-element.6), channel_id=1, replica_groups=mesh['chan'=8,'tm'=4] {'chan'}, dimensions={0}, use_global_device_ids=true | all-gather | bytes 36864 | tf_op jit(solution)/shard_map/all_gather | solution.py:99
  64.0 0.8 convolution_bitcast_fusion.1
  64.8 0.0 reduce-scatter.7.cloned.1.call-update
  64.8 0.0 copy-start
  64.8 0.0 reduce-scatter.5.cloned.1.call-start
  64.9 137.3 %all-gather.2.cloned.1.call-done = bf16[256,64,2,128]{1,0,2,3:T(8,128)(2,1)} async-done(((bf16[32,64,2,128]{1,0,2,3:T(8,128)(2,1)}), bf16[256,64,2,128]{1,0,2,3:T(8,128)(2,1)}) %all-gather.2.cloned.1.call-update) | async-done | bytes 8388624 | tf_op jit(solution)/shard_map/all_gather | solution.py:98
  202.2 9.3 %fusion.59 = (bf16[256,64,1,128]{1,0,2,3:T(8,128)(2,1)S(1)}, bf16[256,64,1,128]{1,0,2,3:T(8,128)(2,1)}) fusion(bf16[256,64,2,128]{1,0,2,3:T(8,128)(2,1)} %all-gather.2.cloned.1.call-done), kind=kLoop, calls=%fused_computation.84 | loop fusion | flops 2097152 | bytes 16777216 | tf_op jit(solution)/shard_map/slice | solution.py:48
  211.5 7.4 %fusion.8 = f32[32,256,1,128]{1,0,3,2:T(8,128)S(1)} fusion(bf16[32,64,2,128]{1,0,2,3:T(8,128)(2,1)S(1)} %copy-done, bf16[256,64,1,128]{1,0,2,3:T(8,128)(2,1)} %get-tuple-element.8, bf16[256,64,1,128]{1,0,2,3:T(8,128)(2,1)S(1)} %get-tuple-element.7), kind=kOutput, calls=%fused_computation.11 | convolution fusion | flops 272629760 | bytes 13631488 | tf_op jit(solution)/shard_map/iscf,jscf->ijf/dot_general | solution.py:52
  218.9 8.4 %convolution_bitcast_fusion = f32[32,256,1,128]{1,0,3,2:T(8,128)S(1)} fusion(bf16[256,64,2,128]{1,0,2,3:T(8,128)(2,1)} %all-gather.2.cloned.1.call-done, bf16[32,64,2,128]{1,0,2,3:T(8,128)(2,1)S(1)} %copy-done), kind=kOutput, calls=%fused_computation.12 | convolution fusion | flops 268435456 | bytes 13631488 | tf_op jit(solution)/shard_map/iscf,jscf->ijf/dot_general | solution.py:49
  227.3 4.1 %pad_maximum_fusion = f32[32,256,2,128]{1,0,3,2:T(8,128)} fusion(f32[32,256,1,128]{1,0,3,2:T(8,128)S(1)} %fusion.8, f32[32,256,1,128]{1,0,3,2:T(8,128)S(1)} %convolution_bitcast_fusion), kind=kLoop, calls=%fused_computation.5 | loop fusion | flops 2097152 | bytes 16777216 | tf_op jit(solution)/shard_map/stack | solution.py:55
  231.4 11.1 %copy.21 = f32[32,256,2,128]{3,0,2,1:T(8,128)} copy(f32[32,256,2,128]{1,0,3,2:T(8,128)} %pad_maximum_fusion) | data formatting | bytes 16777216 | tf_op jit(solution)/shard_map/stack | solution.py:55
  242.4 0.0 reduce-scatter.5.cloned.1.call-update
  242.5 0.5 fusion.43
  243.0 0.0 reduce-scatter.7.cloned.1.call-done
  243.0 0.8 copy.27
  243.9 82.5 %reduce-scatter.5.cloned.1.call-done = f32[32,64,2,128]{3,0,2,1:T(8,128)} async-done(((f32[32,256,2,128]{3,0,2,1:T(8,128)}), f32[32,64,2,128]{3,0,2,1:T(8,128)}) %reduce-scatter.5.cloned.1.call-update) | async-done | bytes 2097168 | tf_op jit(solution)/shard_map/reduce_scatter | solution.py:103
  326.4 4.5 %copy.22 = f32[32,64,2,128]{3,2,1,0:T(2,128)} copy(f32[32,64,2,128]{3,0,2,1:T(8,128)} %reduce-scatter.5.cloned.1.call-done) | data formatting | bytes 4194304 | tf_op jit(solution)/shard_map/reduce_scatter | solution.py:103
  330.9 2.9 reshape.45
  333.9 3.1 convolution_multiply_fusion
  (12 shorter events, 0.0 us)
Async XLA Ops:
  7.4 7.8 %copy-start.3 = (s32[32,64]{1,0:T(8,128)S(1)}, s32[32,64]{1,0:T(8,128)}, u32[]{:S(2)}) copy-start(s32[32,64]{1,0:T(8,128)} %param.5) | copy-start | bytes 24580
  7.4 7.8 %copy-start.4 = (s32[32]{0:T(128)S(1)}, s32[32]{0:T(128)}, u32[]{:S(2)}) copy-start(s32[32]{0:T(128)} %param.4) | copy-start | bytes 388
  7.4 194.8 %all-gather.2.cloned.1.call-start = ((), (), s32[]{:S(2)}) async-start(), calls=%async_computation.2 | async-start | bytes 18874368 | tf_op jit(solution)/shard_map/all_gather | solution.py:98
  7.4 7.9 %copy-start.1 = (f32[32,16384]{1,0:T(8,128)S(1)}, f32[32,16384]{1,0:T(8,128)}, u32[]{:S(2)}) copy-start(f32[32,16384]{1,0:T(8,128)} %param.3) | copy-start | bytes 6291460
  9.4 7.9 %collective-permute-start = (f32[32,64]{1,0:T(8,128)S(1)}, f32[32,64]{1,0:T(8,128)S(1)}, u32[]{:S(2)}, u32[]{:S(2)}) collective-permute-start(f32[32,64]{1,0:T(8,128)S(1)} %get-tuple-element.12), channel_id=1, source_target_pairs={{0,1},{1,2},{2,3},{4,5},{5,6},{6,7},{8,9},{9,10},{10,11},{12,13},{... | collective-permute-start | bytes 24584 | tf_op jit(solution)/shard_map/ppermute | solution.py:19
  13.3 4.5 %collective-permute-start.1 = (f32[32,64]{1,0:T(8,128)S(1)}, f32[32,64]{1,0:T(8,128)S(1)}, u32[]{:S(2)}, u32[]{:S(2)}) collective-permute-start(f32[32,64]{1,0:T(8,128)S(1)} %get-tuple-element.11), channel_id=1, source_target_pairs={{1,0},{2,1},{3,2},{5,4},{6,5},{7,6},{9,8},{10,9},{11,10},{13,12},{... | collective-permute-start | bytes 24584 | tf_op jit(solution)/shard_map/ppermute | solution.py:20
  23.2 1.6 copy-start.2
  47.8 195.2 %reduce-scatter.7.cloned.1.call-start = ((), (), s32[]{:S(2)}) async-start(), calls=%async_computation.4 | async-start | bytes 163840
  64.8 146.7 %copy-start = (bf16[32,64,2,128]{1,0,2,3:T(8,128)(2,1)S(1)}, bf16[32,64,2,128]{1,0,2,3:T(8,128)(2,1)}, u32[]{:S(2)}) copy-start(bf16[32,64,2,128]{1,0,2,3:T(8,128)(2,1)} %multiply_convert_fusion) | copy-start | bytes 3145732
  64.8 261.6 %reduce-scatter.5.cloned.1.call-start = ((), (), s32[]{:S(2)}) async-start(), calls=%async_computation.3 | async-start | bytes 10485760 | tf_op jit(solution)/shard_map/reduce_scatter | solution.py:103
Sparse Core Ops, SparseCore 0:
  48.0 154.1 all-gather.1
Sparse Core Ops, SparseCore 1:
  64.9 24.1 reduce-scatter.6
  242.5 83.8 reduce-scatter.4
where the time goes:
time: 346 us; the launch traced here: 344 us
  waiting for transfers between devices  220 us (64%)
  local copies, waits for them, and re-layouts  37.7 us (11%)
  matrix products  27.8 us (8%)
  other arithmetic  22 us (6%)
  blocking collectives  16.1 us (5%)
  between operations  15 us (4%)
  starting transfers between devices  5.32 us (2%)
    all_gather x1, waiting for transfers between devices, body(): lax.all_gather(whitened, 'chan', axis=0, tiled=True)  137 us
    reduce_scatter x1, waiting for transfers between devices, body(): lax.psum_scatter(cross_all, 'tm', scatter_dimension=1, tiled=True)  82.5 us
    all_gather x1, blocking collectives, body(): lax.all_gather(seg_mask, 'chan', axis=0, tiled=True)  16.1 us
    another operation x1, local copies, waits for them, and re-layouts, make_accumulate(): block_cross = jnp.stack([cross_real, cross_imag], axis=2)  11.1 us
    slice x1, other arithmetic, make_accumulate(): turned = jnp.stack([spec_block[:, :, 1], -spec_block[:, :, 0]], axis=2)  9.34 us
    dot_general x1, matrix products, make_accumulate(): jnp.einsum('iscf,jscf->ijf', local_spec, spec_block, preferred_element_ty...  8.38 us
    dot_general x1, matrix products, make_accumulate(): jnp.einsum('iscf,jscf->ijf', local_spec, turned, preferred_element_type=j...  7.38 us
  transfers between devices with their start and end apart: 5, of which 3 were waited for; matrix products, arithmetic and copies ran while one was open for 13% of the time, Pallas kernels for 0%

commit v1 on v0

v1 whole, which is shorter than its diff:
```python
import functools

import jax
import jax.numpy as jnp
import numpy as np
from jax import lax
from jax.experimental import pallas as pl
from jax.experimental.pallas import tpu as pltpu
from jax.sharding import PartitionSpec as P

SEG_LEN = 256
BINS = 128
HALF_WIN = 64
SMOOTH = 4
ROWS = 2 * BINS
LANES = 128
SUB = 16
CHAN_ROWS = 32
SEGS = 64
PER_LANE = LANES // CHAN_ROWS
MESH = pl.DeviceIdType.MESH


def split_table(table):
    high = table.astype(jnp.bfloat16)
    low = (table - high.astype(np.float32)).astype(jnp.bfloat16)
    return high, low


def make_tables():
    row_bin = np.arange(ROWS) // 2
    row_imag = np.arange(ROWS) % 2 == 1
    time = np.arange(SEG_LEN)
    phase = 2.0 * np.pi / SEG_LEN * (row_bin[:, None] * time[None, :] % SEG_LEN)
    forward = np.where(row_imag[:, None], -np.sin(phase), np.cos(phase)).astype(np.float32)
    lag = np.arange(SEG_LEN) - BINS
    back = 2.0 * np.pi / SEG_LEN * (row_bin[:, None] * lag[None, :] % SEG_LEN)
    inverse = np.where(row_imag[:, None], -np.sin(back), np.cos(back))
    inverse = (inverse * (row_bin > 0)[:, None]).astype(np.float32)
    smooth = np.abs(row_bin[:, None] - row_bin[None, :]) <= SMOOTH
    sample_in = np.arange(2 * SEG_LEN)[:, None] - SEG_LEN // 2
    sample_out = np.arange(SEG_LEN)[None, :]
    box = np.abs(sample_in - sample_out) <= HALF_WIN
    return (
        split_table(forward),
        split_table(inverse),
        smooth.astype(jnp.bfloat16),
        box.astype(jnp.bfloat16),
    )


def halves(value):
    high = value.astype(jnp.bfloat16)
    return high, (value - high.astype(jnp.float32)).astype(jnp.bfloat16)


def mm(a, b, dims=((1,), (0,))):
    return lax.dot_general(a, b, (dims, ((), ())), preferred_element_type=jnp.float32)


NT = ((1,), (1,))
TN = ((0,), (0,))


def spread_kernel(
    n_chan, n_tm,
    x_hbm, mask_ref, box_ref, fwd_hi, fwd_lo, smooth_ref,
    out_hbm,
    xpad, turned, send1, recv1, pair, cross, send2,
    halo_send, halo_recv, local_sem, send1_sem, recv1_sem, send2_sem, recv2_sem,
):
    n = n_chan * n_tm
    span = SEGS * SEG_LEN
    chunk = ROWS // n
    chan, tm = lax.axis_index("chan"), lax.axis_index("tm")
    me = chan * n_tm + tm

    def device(index):
        return {"chan": index // n_tm, "tm": lax.rem(index, n_tm)}

    fill = pltpu.make_async_copy(x_hbm, xpad.at[:, pl.ds(LANES, span)], local_sem.at[0])
    fill.start()

    barrier = pltpu.get_barrier_semaphore()

    def greet(k, _):
        pl.semaphore_signal(
            barrier, inc=1, device_id=device(lax.rem(me + k, n)), device_id_type=MESH
        )
        return 0

    lax.fori_loop(1, n, greet, 0)
    pl.semaphore_wait(barrier, n - 1)

    to_left = pltpu.make_async_remote_copy(
        src_ref=x_hbm.at[:, pl.ds(0, LANES)],
        dst_ref=xpad.at[:, pl.ds(LANES + span, LANES)],
        send_sem=halo_send.at[0], recv_sem=halo_recv.at[0],
        device_id={"chan": chan, "tm": jnp.maximum(tm - 1, 0)}, device_id_type=MESH,
    )
    to_right = pltpu.make_async_remote_copy(
        src_ref=x_hbm.at[:, pl.ds(span - LANES, LANES)],
        dst_ref=xpad.at[:, pl.ds(0, LANES)],
        send_sem=halo_send.at[1], recv_sem=halo_recv.at[1],
        device_id={"chan": chan, "tm": jnp.minimum(tm + 1, n_tm - 1)}, device_id_type=MESH,
    )
    has_left, has_right = tm > 0, tm < n_tm - 1

    @pl.when(has_left)
    def _():
        to_left.start()

    @pl.when(has_right)
    def _():
        to_right.start()

    @pl.when(jnp.logical_not(has_left))
    def _():
        xpad[:, 0:LANES] = jnp.zeros((CHAN_ROWS, LANES), jnp.float32)

    @pl.when(jnp.logical_not(has_right))
    def _():
        xpad[:, LANES + span : 2 * LANES + span] = jnp.zeros((CHAN_ROWS, LANES), jnp.float32)

    row = lax.broadcasted_iota(jnp.int32, (ROWS, 2 * LANES), 0)

    def whiten(m):
        window = jnp.concatenate(
            [
                xpad[:, pl.ds(pl.multiple_of(m * 8 * SEG_LEN + i * SEG_LEN, LANES), 2 * SEG_LEN)]
                for i in range(8)
            ],
            axis=0,
        )
        high, low = halves(jnp.abs(window))
        level = (mm(high, box_ref[...]) + mm(low, box_ref[...])) * (1.0 / (2 * HALF_WIN + 1))
        normed = window[:, SEG_LEN // 2 : SEG_LEN // 2 + SEG_LEN] / (level + 1e-5)
        high, low = halves(normed)
        spectrum = (
            mm(fwd_hi[...], high, NT) + mm(fwd_hi[...], low, NT) + mm(fwd_lo[...], high, NT)
        )
        power = spectrum * spectrum
        high, low = halves(power)
        smoothed = (mm(smooth_ref[...], high) + mm(smooth_ref[...], low)) * (
            1.0 / (2 * SMOOTH + 1)
        )
        mean_power = jnp.sum(power, axis=0, keepdims=True) * (1.0 / BINS)
        mask = jnp.concatenate(
            [mask_ref[pl.ds(2 * m, 1), :], mask_ref[pl.ds(2 * m + 1, 1), :]], axis=1
        )
        whitened = spectrum * (mask * lax.rsqrt(smoothed + (0.1 * mean_power + 1e-6)))
        whitened = jnp.where(row == 0, mask, jnp.where(row == 1, 0.0, whitened))
        for u in range(2):
            turned[pl.ds(pl.multiple_of((2 * m + u) * ROWS, ROWS), ROWS), :] = whitened[
                :, u * LANES : (u + 1) * LANES
            ]

    fill.wait()

    def inner(m, _):
        whiten(m)
        return 0

    last = SEGS // 8 - 1
    lax.fori_loop(1, last, inner, 0)

    @pl.when(has_left)
    def _():
        to_left.wait_send()
        to_right.wait_recv()

    @pl.when(has_right)
    def _():
        to_right.wait_send()
        to_left.wait_recv()

    def outer(m, _):
        whiten(m * last)
        return 0

    lax.fori_loop(0, 2, outer, 0)

    def turn(step, _):
        for i in range(8):
            r = step * 8 + i
            send1[r] = turned[pl.ds(r, SUB, stride=ROWS), :].astype(jnp.bfloat16)
        return 0

    lax.fori_loop(0, ROWS // 8, turn, 0)

    def exchange(source, target, send_sem, recv_sem, local):
        def part(index):
            return source.at[pl.ds(index * chunk, chunk)]

        def out_copy(to):
            return pltpu.make_async_remote_copy(
                src_ref=part(to), dst_ref=target.at[pl.ds(me * chunk, chunk)],
                send_sem=send_sem.at[to], recv_sem=recv_sem.at[me],
                device_id=device(to), device_id_type=MESH,
            )

        def in_copy(frm):
            return pltpu.make_async_remote_copy(
                src_ref=part(frm), dst_ref=target.at[pl.ds(frm * chunk, chunk)],
                send_sem=send_sem.at[frm], recv_sem=recv_sem.at[frm],
                device_id=device(frm), device_id_type=MESH,
            )

        own = pltpu.make_async_copy(part(me), target.at[pl.ds(me * chunk, chunk)], local)

        def start(k, _):
            out_copy(lax.rem(me + k, n)).start()
            return 0

        def arrive(k, _):
            in_copy(lax.rem(me + n - k, n)).wait_recv()
            return 0

        def leave(k, _):
            out_copy(lax.rem(me + k, n)).wait_send()
            return 0

        lax.fori_loop(1, n, start, 0)
        own.start()
        own.wait()
        lax.fori_loop(1, n, arrive, 0)
        return lambda: lax.fori_loop(1, n, leave, 0)

    left1 = exchange(send1, recv1, send1_sem, recv1_sem, local_sem.at[1])

    lane = lax.broadcasted_iota(jnp.int32, (SUB, LANES), 1)
    low_half = lane < LANES // 2
    even = lax.rem(lane // CHAN_ROWS, 2) == 0
    n_all = n_chan * CHAN_ROWS
    half_k = n_tm * SEGS

    def swap(first, second, distance, keep):
        return (
            jnp.where(keep, first, pltpu.roll(second, distance, 1)),
            jnp.where(keep, pltpu.roll(first, LANES - distance, 1), second),
        )

    def one_bin(f, _):
        for c in range(2):
            for b in range(n_tm):
                for g in range(n_chan // PER_LANE):
                    tiles = [
                        recv1[((g * PER_LANE + i) * n_tm + b) * chunk + 2 * f + c].astype(
                            jnp.float32
                        )
                        for i in range(PER_LANE)
                    ]
                    p0, p2 = swap(tiles[0], tiles[2], 64, low_half)
                    p1, p3 = swap(tiles[1], tiles[3], 64, low_half)
                    u0, u1 = swap(p0, p1, 32, even)
                    u2, u3 = swap(p2, p3, 32, even)
                    for q, value in enumerate((u0, u1, u2, u3)):
                        at = b * SEGS + q * SUB
                        pair[c * half_k + at : c * half_k + at + SUB, g * LANES : (g + 1) * LANES] = (
                            value.astype(jnp.bfloat16)
                        )
                        other = (1 - c) * half_k + at
                        pair[other : other + SUB, n_all + g * LANES : n_all + (g + 1) * LANES] = (
                            value if c == 1 else -value
                        ).astype(jnp.bfloat16)
        cross[...] = mm(pair[:, :n_all], pair[...], TN)
        counts = jnp.logical_and(me == 0, f == 0)
        for a in range(n_chan):
            for p in range(n_tm // 2):
                tops = []
                for c in range(2):
                    at = c * n_all + p * LANES
                    top = cross[a * CHAN_ROWS : a * CHAN_ROWS + SUB, at : at + LANES]
                    bottom = cross[a * CHAN_ROWS + SUB : (a + 1) * CHAN_ROWS, at : at + LANES]
                    tops.append(swap(top, bottom, 64, low_half))
                for i in range(2):
                    dest = (a * n_tm + 2 * p + i) * chunk + 2 * f
                    real = tops[0][i].astype(jnp.bfloat16)
                    rest = tops[0][i] - real.astype(jnp.float32)
                    send2[dest] = real
                    send2[dest + 1] = jnp.where(counts, rest, tops[1][i]).astype(jnp.bfloat16)
        return 0

    lax.fori_loop(0, chunk // 2, one_bin, 0)
    left2 = exchange(send2, out_hbm, send2_sem, recv2_sem, local_sem.at[2])
    left1()
    left2()


def lag_kernel(steps, cross_ref, inv_hi, inv_lo, out_ref, rows):
    step = pl.program_id(0)

    @pl.when(step == 0)
    def _():
        count = cross_ref[0].astype(jnp.float32) + cross_ref[1].astype(jnp.float32)
        scale = 2.0 / jnp.maximum(count, 1.0)

        def turn(block, _):
            for i in range(8):
                r = block * 8 + i
                rows[pl.ds(r, SUB, stride=ROWS), :] = cross_ref[r].astype(jnp.float32) * scale
            return 0

        lax.fori_loop(0, ROWS // 8, turn, 0)

    for i in range(SUB // steps):
        at = pl.multiple_of((step * (SUB // steps) + i) * ROWS, ROWS)
        high, low = halves(rows[pl.ds(at, ROWS), :])
        lagged = mm(high, inv_hi[...], TN) + mm(low, inv_hi[...], TN) + mm(high, inv_lo[...], TN)
        out_ref[0, i] = lagged[: LANES // 2]
        out_ref[1, i] = lagged[LANES // 2 :]


def body(n_chan, n_tm, traces, live_channel, valid_segment):
    (fwd_hi, fwd_lo), (inv_hi, inv_lo), smooth, box = make_tables()
    n = n_chan * n_tm
    n_all = n_chan * CHAN_ROWS
    span = traces.shape[1]
    mask = (live_channel[:, None] * valid_segment).astype(jnp.float32)
    mask = mask.T.reshape(SUB, LANES)
    vmem = pl.BlockSpec(memory_space=pltpu.VMEM)
    hbm = pl.BlockSpec(memory_space=pl.ANY)
    dma = pltpu.SemaphoreType.DMA
    tiles = (ROWS, SUB, LANES)
    crossed = pl.pallas_call(
        functools.partial(spread_kernel, n_chan, n_tm),
        out_shape=jax.ShapeDtypeStruct(tiles, jnp.bfloat16),
        in_specs=[hbm] + [vmem] * 5,
        out_specs=hbm,
        scratch_shapes=[
            pltpu.VMEM((CHAN_ROWS, span + 2 * LANES), jnp.float32),
            pltpu.VMEM((SUB * ROWS, LANES), jnp.float32),
            pltpu.VMEM(tiles, jnp.bfloat16),
            pltpu.VMEM(tiles, jnp.bfloat16),
            pltpu.VMEM((2 * n_tm * SEGS, 2 * n_all), jnp.bfloat16),
            pltpu.VMEM((n_all, 2 * n_all), jnp.float32),
            pltpu.VMEM(tiles, jnp.bfloat16),
            dma((2,)), dma((2,)), dma((3,)), dma((n,)), dma((n,)), dma((n,)), dma((n,)),
        ],
        compiler_params=pltpu.CompilerParams(
            collective_id=0, has_side_effects=True, vmem_limit_bytes=40 * 1024 * 1024
        ),
        name="spread",
    )(traces, mask, box, fwd_hi, fwd_lo, smooth)
    steps = 4
    whole = pl.BlockSpec((ROWS, SEG_LEN), lambda i: (0, 0))
    lagged = pl.pallas_call(
        functools.partial(lag_kernel, steps),
        out_shape=jax.ShapeDtypeStruct((2, SUB, LANES // 2, SEG_LEN), jnp.float32),
        grid=(steps,),
        in_specs=[pl.BlockSpec(tiles, lambda i: (0, 0, 0)), whole, whole],
        out_specs=pl.BlockSpec((2, SUB // steps, LANES // 2, SEG_LEN), lambda i: (0, i, 0, 0)),
        scratch_shapes=[pltpu.VMEM((SUB * ROWS, LANES), jnp.float32)],
        compiler_params=pltpu.CompilerParams(vmem_limit_bytes=32 * 1024 * 1024),
        name="lags",
    )(crossed, inv_hi, inv_lo)
    return lagged.reshape(CHAN_ROWS, LANES // 2, SEG_LEN)


def solution(mesh):
    n_chan, n_tm = mesh.shape["chan"], mesh.shape["tm"]
    return jax.shard_map(
        functools.partial(body, n_chan, n_tm),
        mesh=mesh,
        in_specs=(P("chan", "tm"), P("chan"), P("chan", "tm")),
        out_specs=P("chan", "tm", None),
        check_vma=False,
    )
```

time: 346 us -> 75.9 us (0.22)
  the two profiles are of different devices: /device:TPU:1 before, /device:TPU:25 now
where the time goes in v1:
time: 75.9 us; the launch traced here: 75.7 us
  Pallas kernels  69.4 us (91%)
  local copies, waits for them, and re-layouts  5.42 us (7%)
  other arithmetic  0.79 us (1%)
    pallas_call x1, Pallas kernels, body(): pl.pallas_call(functools.partial(spread_kernel, n_chan, n_tm), out_shape=...  64.8 us
    unnamed x14, local copies, waits for them, and re-layouts  5.27 us
    pallas_call x1, Pallas kernels, body(): pl.pallas_call(functools.partial(lag_kernel, steps), out_shape=jax.ShapeD...  4.64 us

profile of v1, /device:TPU:25, one launch (start us, length us, event | category | flops | bytes accessed | tf_op | source)
XLA Modules:
  0.0 75.7 jit_solution(10649316936287402341)
XLA Ops:
  0.0 0.8 %convert_bitcast_fusion = f32[64,32]{0,1:T(8,128)S(1)} fusion(s32[32,64]{1,0:T(8,128)} %param.11, s32[32]{0:T(128)} %param.10), kind=kLoop, calls=%fused_computation | loop fusion | flops 4096 | bytes 16512 | tf_op jit(solution)/shard_map/transpose | solution.py:320
  0.8 0.1 copy.11
  0.9 0.1 reshape.7.mask_ref
  0.9 0.0 copy-start
  0.9 1.6 %copy-done = f32[32,16384]{1,0:T(8,128)S(1)} copy-done((f32[32,16384]{1,0:T(8,128)S(1)}, f32[32,16384]{1,0:T(8,128)}, u32[]{:S(2)}) %copy-start) | copy-done | bytes 2097176
  2.5 0.0 copy-start.1
  2.6 0.9 %copy-done.1 = bf16[512,256]{1,0:T(8,128)(2,1)S(1)} copy-done((bf16[512,256]{1,0:T(8,128)(2,1)S(1)}, bf16[512,256]{1,0:T(8,128)(2,1)}, u32[]{:S(2)}) %copy-start.1) | copy-done | bytes 262168
  3.5 0.0 copy-start.4
  3.5 0.9 %copy-done.4 = bf16[256,256]{1,0:T(8,128)(2,1)S(1)} copy-done((bf16[256,256]{1,0:T(8,128)(2,1)S(1)}, bf16[256,256]{1,0:T(8,128)(2,1)}, u32[]{:S(2)}) %copy-start.4) | copy-done | bytes 131096
  4.4 0.0 copy-start.5
  4.4 0.9 %copy-done.5 = bf16[256,256]{1,0:T(8,128)(2,1)S(1)} copy-done((bf16[256,256]{1,0:T(8,128)(2,1)S(1)}, bf16[256,256]{1,0:T(8,128)(2,1)}, u32[]{:S(2)}) %copy-start.5) | copy-done | bytes 131096
  5.3 0.0 copy-start.6
  5.3 0.9 %copy-done.6 = bf16[256,256]{1,0:T(8,128)(2,1)S(1)} copy-done((bf16[256,256]{1,0:T(8,128)(2,1)S(1)}, bf16[256,256]{1,0:T(8,128)(2,1)}, u32[]{:S(2)}) %copy-start.6) | copy-done | bytes 131096
  6.2 0.0 copy-start.2
  6.2 0.0 copy-start.3
  6.2 64.8 %spread.1.cross_ref = bf16[256,16,128]{2,1,0:T(8,128)(2,1)S(1)} custom-call(f32[32,16384]{1,0:T(8,128)S(1)} %copy-done, f32[16,128]{1,0:T(8,128)S(1)} %reshape.7.mask_ref, bf16[512,256]{1,0:T(8,128)(2,1)S(1)} %copy-done.1, bf16[256,256]{1,0:T(8,128)(2,1)S(1)} %copy-done.6, bf16[256,256]{1,0:T(8,128)(2,1)S(1)} %copy-done.5, bf16[256,256]{1,0:T(8,128)(2,1)S(1)} %copy-done.4), custom_call_target="tpu_custom_call" | custom-call | tf_op jit(solution)/shard_map/spread/pallas_call | solution.py:325
  71.0 0.0 copy-done.2
  71.0 0.0 copy-done.3
  71.0 4.6 %lags.1 = f32[2,16,64,256]{3,2,1,0:T(8,128)} custom-call(bf16[256,16,128]{2,1,0:T(8,128)(2,1)S(1)} %spread.1.cross_ref, bf16[256,256]{1,0:T(8,128)(2,1)S(1)} %copy-done.3, bf16[256,256]{1,0:T(8,128)(2,1)S(1)} %copy-done.2), custom_call_target="tpu_custom_call" | custom-call | tf_op jit(solution)/shard_map/lags/pallas_call | solution.py:347
Async XLA Ops:
  0.9 1.6 %copy-start = (f32[32,16384]{1,0:T(8,128)S(1)}, f32[32,16384]{1,0:T(8,128)}, u32[]{:S(2)}) copy-start(f32[32,16384]{1,0:T(8,128)} %x_hbm.1) | copy-start | bytes 6291460
  2.5 0.9 %copy-start.1 = (bf16[512,256]{1,0:T(8,128)(2,1)S(1)}, bf16[512,256]{1,0:T(8,128)(2,1)}, u32[]{:S(2)}) copy-start(bf16[512,256]{1,0:T(8,128)(2,1)} %constant.12.clone.box_ref) | copy-start | bytes 786436
  3.5 0.9 %copy-start.4 = (bf16[256,256]{1,0:T(8,128)(2,1)S(1)}, bf16[256,256]{1,0:T(8,128)(2,1)}, u32[]{:S(2)}) copy-start(bf16[256,256]{1,0:T(8,128)(2,1)} %constant.15.clone.smooth_ref) | copy-start | bytes 393220
  4.4 0.9 %copy-start.5 = (bf16[256,256]{1,0:T(8,128)(2,1)S(1)}, bf16[256,256]{1,0:T(8,128)(2,1)}, u32[]{:S(2)}) copy-start(bf16[256,256]{1,0:T(8,128)(2,1)} %constant.14.clone.fwd_lo) | copy-start | bytes 393220
  5.3 0.9 %copy-start.6 = (bf16[256,256]{1,0:T(8,128)(2,1)S(1)}, bf16[256,256]{1,0:T(8,128)(2,1)}, u32[]{:S(2)}) copy-start(bf16[256,256]{1,0:T(8,128)(2,1)} %constant.13.clone.fwd_hi) | copy-start | bytes 393220
  6.2 64.8 %copy-start.2 = (bf16[256,256]{1,0:T(8,128)(2,1)S(1)}, bf16[256,256]{1,0:T(8,128)(2,1)}, u32[]{:S(2)}) copy-start(bf16[256,256]{1,0:T(8,128)(2,1)} %constant.17.clone.inv_lo) | copy-start | bytes 393220
  6.2 64.8 %copy-start.3 = (bf16[256,256]{1,0:T(8,128)(2,1)S(1)}, bf16[256,256]{1,0:T(8,128)(2,1)}, u32[]{:S(2)}) copy-start(bf16[256,256]{1,0:T(8,128)(2,1)} %constant.16.clone.inv_hi) | copy-start | bytes 393220

commit v2 on v1

v2 whole, which is shorter than its diff:
```python
import functools

import jax
import jax.numpy as jnp
import numpy as np
from jax import lax
from jax.experimental import pallas as pl
from jax.experimental.pallas import tpu as pltpu
from jax.sharding import PartitionSpec as P

SEG_LEN = 256
BINS = 128
HALF_WIN = 64
SMOOTH = 4
ROWS = 2 * BINS
LANES = 128
SUB = 16
CHAN_ROWS = 32
SEGS = 64
PER_LANE = LANES // CHAN_ROWS
MESH = pl.DeviceIdType.MESH


def split_table(table):
    high = table.astype(jnp.bfloat16)
    low = (table - high.astype(np.float32)).astype(jnp.bfloat16)
    return high, low


def make_tables():
    row_bin = np.arange(ROWS) // 2
    row_imag = np.arange(ROWS) % 2 == 1
    time = np.arange(SEG_LEN)
    phase = 2.0 * np.pi / SEG_LEN * (row_bin[:, None] * time[None, :] % SEG_LEN)
    forward = np.where(row_imag[:, None], -np.sin(phase), np.cos(phase)).astype(np.float32)
    lag = np.arange(SEG_LEN) - BINS
    back = 2.0 * np.pi / SEG_LEN * (row_bin[:, None] * lag[None, :] % SEG_LEN)
    inverse = np.where(row_imag[:, None], -np.sin(back), np.cos(back))
    inverse = (inverse * (row_bin > 0)[:, None]).astype(np.float32)
    smooth = np.abs(row_bin[:, None] - row_bin[None, :]) <= SMOOTH
    sample_in = np.arange(2 * SEG_LEN)[:, None] - SEG_LEN // 2
    sample_out = np.arange(SEG_LEN)[None, :]
    box = np.abs(sample_in - sample_out) <= HALF_WIN
    return (
        split_table(forward),
        split_table(inverse),
        smooth.astype(jnp.bfloat16),
        box.astype(jnp.bfloat16),
    )


def halves(value):
    high = value.astype(jnp.bfloat16)
    return high, (value - high.astype(jnp.float32)).astype(jnp.bfloat16)


def mm(a, b, dims=((1,), (0,))):
    return lax.dot_general(a, b, (dims, ((), ())), preferred_element_type=jnp.float32)


NT = ((1,), (1,))
TN = ((0,), (0,))


def spread_kernel(
    n_chan, n_tm, piece,
    x_hbm, table_hbm, live_ref, valid_ref,
    out_hbm,
    xpad, tables, mask_rows, turned, send1, recv1, pair, cross, send2,
    halo_send, halo_recv, local_sem, send1_sem, recv1_sem, send2_sem, recv2_sem,
):
    n = n_chan * n_tm
    span = SEGS * SEG_LEN
    bins = BINS // n
    pieces = bins // piece
    chan, tm = lax.axis_index("chan"), lax.axis_index("tm")
    me = chan * n_tm + tm

    def device(index):
        return {"chan": index // n_tm, "tm": lax.rem(index, n_tm)}

    load = pltpu.make_async_copy(table_hbm, tables, local_sem.at[1])
    load.start()
    fill = pltpu.make_async_copy(x_hbm, xpad.at[:, pl.ds(LANES, span)], local_sem.at[0])
    fill.start()

    barrier = pltpu.get_barrier_semaphore()

    def greet(k, _):
        pl.semaphore_signal(
            barrier, inc=1, device_id=device(lax.rem(me + k, n)), device_id_type=MESH
        )
        return 0

    lax.fori_loop(1, n, greet, 0)

    to_left = pltpu.make_async_remote_copy(
        src_ref=x_hbm.at[:, pl.ds(0, LANES)],
        dst_ref=xpad.at[:, pl.ds(LANES + span, LANES)],
        send_sem=halo_send.at[0], recv_sem=halo_recv.at[0],
        device_id={"chan": chan, "tm": jnp.maximum(tm - 1, 0)}, device_id_type=MESH,
    )
    to_right = pltpu.make_async_remote_copy(
        src_ref=x_hbm.at[:, pl.ds(span - LANES, LANES)],
        dst_ref=xpad.at[:, pl.ds(0, LANES)],
        send_sem=halo_send.at[1], recv_sem=halo_recv.at[1],
        device_id={"chan": chan, "tm": jnp.minimum(tm + 1, n_tm - 1)}, device_id_type=MESH,
    )
    has_left, has_right = tm > 0, tm < n_tm - 1

    @pl.when(jnp.logical_not(has_left))
    def _():
        xpad[:, 0:LANES] = jnp.zeros((CHAN_ROWS, LANES), jnp.float32)

    @pl.when(jnp.logical_not(has_right))
    def _():
        xpad[:, LANES + span : 2 * LANES + span] = jnp.zeros((CHAN_ROWS, LANES), jnp.float32)

    valid = valid_ref[...].astype(jnp.float32).astype(jnp.bfloat16)
    live = live_ref[...].astype(jnp.float32)
    mask_sum = jnp.zeros((SUB, LANES), jnp.float32)
    seg_row = lax.broadcasted_iota(jnp.int32, (SUB, SEGS), 0) * PER_LANE
    seg_col = lax.broadcasted_iota(jnp.int32, (SUB, SEGS), 1)
    chan_row = lax.broadcasted_iota(jnp.int32, (CHAN_ROWS, LANES), 0)
    chan_lane = lax.broadcasted_iota(jnp.int32, (CHAN_ROWS, LANES), 1)
    for q in range(PER_LANE):
        pick = (seg_col == seg_row + q).astype(jnp.float32).astype(jnp.bfloat16)
        place = (chan_lane == chan_row + q * CHAN_ROWS).astype(jnp.float32).astype(jnp.bfloat16)
        picked = (mm(pick, valid, NT) * live).astype(jnp.bfloat16)
        mask_sum = mask_sum + mm(picked, place)
    mask_rows[...] = mask_sum

    pl.semaphore_wait(barrier, n - 1)

    @pl.when(has_left)
    def _():
        to_left.start()

    @pl.when(has_right)
    def _():
        to_right.start()

    row = lax.broadcasted_iota(jnp.int32, (ROWS, 2 * LANES), 0)

    def whiten(m, slot):
        window = jnp.concatenate(
            [
                xpad[:, pl.ds(pl.multiple_of(m * 8 * SEG_LEN + i * SEG_LEN, LANES), 2 * SEG_LEN)]
                for i in range(8)
            ],
            axis=0,
        )
        box = tables[3 * ROWS : 5 * ROWS]
        high, low = halves(jnp.abs(window))
        level = (mm(high, box) + mm(low, box)) * (1.0 / (2 * HALF_WIN + 1))
        normed = window[:, SEG_LEN // 2 : SEG_LEN // 2 + SEG_LEN] / (level + 1e-5)
        high, low = halves(normed)
        fwd_hi = tables[0:ROWS]
        spectrum = mm(fwd_hi, high, NT) + mm(fwd_hi, low, NT) + mm(tables[ROWS : 2 * ROWS], high, NT)
        power = spectrum * spectrum
        high, low = halves(power)
        smooth = tables[2 * ROWS : 3 * ROWS]
        smoothed = (mm(smooth, high) + mm(smooth, low)) * (1.0 / (2 * SMOOTH + 1))
        mean_power = jnp.sum(power, axis=0, keepdims=True) * (1.0 / BINS)
        mask = jnp.concatenate(
            [mask_rows[pl.ds(2 * m, 1), :], mask_rows[pl.ds(2 * m + 1, 1), :]], axis=1
        )
        whitened = spectrum * (mask * lax.rsqrt(smoothed + (0.1 * mean_power + 1e-6)))
        whitened = jnp.where(row == 0, mask, jnp.where(row == 1, 0.0, whitened))
        for u in range(2):
            turned[pl.ds(pl.multiple_of((2 * slot + u) * ROWS, ROWS), ROWS), :] = whitened[
                :, u * LANES : (u + 1) * LANES
            ]

    def exchange(source, target, size, place, send_sem, recv_sem, sems, local):
        def copy(part, spot, to, at):
            return pltpu.make_async_remote_copy(
                src_ref=source.at[pl.ds(place(part), size)],
                dst_ref=target.at[pl.ds(place(spot), size)],
                send_sem=send_sem.at[sems + to], recv_sem=recv_sem.at[sems + at],
                device_id=device(to), device_id_type=MESH,
            )

        own = pltpu.make_async_copy(
            source.at[pl.ds(place(me), size)], target.at[pl.ds(place(me), size)], local
        )

        def start():
            def one(k, _):
                to = lax.rem(me + k, n)
                copy(to, me, to, me).start()
                return 0

            lax.fori_loop(1, n, one, 0)
            own.start()

        def arrive(frm):
            copy(frm, frm, frm, frm).wait_recv()

        def leave():
            def one(k, _):
                to = lax.rem(me + k, n)
                copy(to, me, to, me).wait_send()
                return 0

            lax.fori_loop(1, n, one, 0)

        return start, own.wait, arrive, leave

    def spread(h):
        return exchange(
            send1, recv1, bins, lambda d: h * BINS + d * bins,
            send1_sem, recv1_sem, h * n, local_sem.at[2 + h],
        )

    fill.wait()
    load.wait()

    def half(h, _):
        def two(p, _):
            @pl.when(jnp.logical_and(h + p == 1, jnp.logical_and(p == 1, has_left)))
            def _():
                to_left.wait_send()
                to_right.wait_recv()

            @pl.when(jnp.logical_and(h + p == 2, has_right))
            def _():
                to_right.wait_send()
                to_left.wait_recv()

            first = jnp.where(h == 0, 1 + 2 * p, 4 + 2 * p)
            second = jnp.where(h == 0, 2 - 2 * p, 5 + 2 * p)
            whiten(first, first - 4 * h)
            whiten(second, second - 4 * h)
            return 0

        lax.fori_loop(0, 2, two, 0)

        def turn(step, _):
            for i in range(8):
                f = step * 8 + i
                tile = jnp.concatenate(
                    [turned[pl.ds(2 * f + c, SUB // 2, stride=ROWS), :] for c in range(2)], axis=0
                )
                send1[h * BINS + f] = tile.astype(jnp.bfloat16)
            return 0

        lax.fori_loop(0, BINS // 8, turn, 0)
        spread(h)[0]()
        return 0

    lax.fori_loop(0, 2, half, 0)

    lane = lax.broadcasted_iota(jnp.int32, (SUB, LANES), 1)
    low_half = lane < LANES // 2
    even = lax.rem(lane // CHAN_ROWS, 2) == 0
    n_all = n_chan * CHAN_ROWS
    depth = 2 * n_tm * SEGS
    groups = n_chan // PER_LANE

    def swap(first, second, distance, keep):
        return (
            jnp.where(keep, first, pltpu.roll(second, distance, 1)),
            jnp.where(keep, pltpu.roll(first, LANES - distance, 1), second),
        )

    def gather(h, _):
        _, own_wait, arrive, _ = spread(h)
        own_wait()

        def group(j, _):
            b = lax.rem(j, n_tm)
            g = lax.rem(chan // PER_LANE + j // n_tm, groups)
            sources = [(g * PER_LANE + i) * n_tm + b for i in range(PER_LANE)]
            for source in sources:
                @pl.when(source != me)
                def _():
                    arrive(source)

            for f in range(bins):
                tiles = [
                    recv1[h * BINS + source * bins + f].astype(jnp.float32) for source in sources
                ]
                p0, p2 = swap(tiles[0], tiles[2], 64, low_half)
                p1, p3 = swap(tiles[1], tiles[3], 64, low_half)
                u0, u1 = swap(p0, p1, 32, even)
                u2, u3 = swap(p2, p3, 32, even)
                for q, value in enumerate((u0, u1, u2, u3)):
                    at = pl.multiple_of(
                        f * depth + ((h * n_tm + b) * PER_LANE + q) * SUB, SUB
                    )
                    left = pl.multiple_of(g * LANES, LANES)
                    right = pl.multiple_of(n_all + g * LANES, LANES)
                    other = jnp.concatenate([value[SUB // 2 :], -value[: SUB // 2]], axis=0)
                    pair[pl.ds(at, SUB), pl.ds(left, LANES)] = value.astype(jnp.bfloat16)
                    pair[pl.ds(at, SUB), pl.ds(right, LANES)] = other.astype(jnp.bfloat16)
            return 0

        lax.fori_loop(0, n // PER_LANE, group, 0)
        return 0

    lax.fori_loop(0, 2, gather, 0)

    def back(s):
        return exchange(
            send2, out_hbm, 2 * piece, lambda d: (d * bins + s * piece) * 2,
            send2_sem, recv2_sem, s * n, local_sem.at[4 + s],
        )

    def some_bins(s, _):
        for i in range(piece):
            at = pl.multiple_of((s * piece + i) * depth, depth)
            cross[i] = mm(pair[pl.ds(at, depth), :n_all], pair[pl.ds(at, depth), :], TN)
        for i in range(piece):
            f = s * piece + i
            counts = jnp.logical_and(me == 0, f == 0)
            for a in range(n_chan):
                for p in range(n_tm // 2):
                    tops = []
                    for c in range(2):
                        at = c * n_all + p * LANES
                        top = cross[i, a * CHAN_ROWS : a * CHAN_ROWS + SUB, at : at + LANES]
                        bottom = cross[
                            i, a * CHAN_ROWS + SUB : (a + 1) * CHAN_ROWS, at : at + LANES
                        ]
                        tops.append(swap(top, bottom, 64, low_half))
                    for e in range(2):
                        dest = ((a * n_tm + 2 * p + e) * bins + f) * 2
                        real = tops[0][e].astype(jnp.bfloat16)
                        imag = tops[1][e]
                        if i == 0:
                            rest = tops[0][e] - real.astype(jnp.float32)
                            imag = jnp.where(counts, rest, imag)
                        send2[dest] = real
                        send2[dest + 1] = imag.astype(jnp.bfloat16)
        back(s)[0]()
        return 0

    lax.fori_loop(0, pieces, some_bins, 0)

    def finish(s, _):
        _, own_wait, arrive, leave = back(s)
        own_wait()

        def one(k, _):
            arrive(lax.rem(me + n - k, n))
            return 0

        lax.fori_loop(1, n, one, 0)
        leave()
        return 0

    lax.fori_loop(0, pieces, finish, 0)

    def done(h, _):
        spread(h)[3]()
        return 0

    lax.fori_loop(0, 2, done, 0)


def lag_kernel(steps, cross_ref, inverse_ref, out_ref, rows, scale):
    step = pl.program_id(0)

    @pl.when(step == 0)
    def _():
        count = cross_ref[0].astype(jnp.float32) + cross_ref[1].astype(jnp.float32)
        scale[...] = (2.0 / jnp.maximum(count, 1.0)).T

        def turn(block, _):
            for i in range(16):
                r = block * 16 + i
                rows[pl.ds(r, SUB, stride=ROWS), :] = cross_ref[r].astype(jnp.float32)
            return 0

        lax.fori_loop(0, ROWS // 16, turn, 0)

    column = lax.broadcasted_iota(jnp.int32, (LANES, SUB), 1)
    for i in range(SUB // steps):
        index = step * (SUB // steps) + i
        value = rows[pl.ds(pl.multiple_of(index * ROWS, ROWS), ROWS), :].astype(jnp.bfloat16)
        lagged = mm(value, inverse_ref[:ROWS], TN) + mm(value, inverse_ref[ROWS:], TN)
        lagged = lagged * jnp.sum(
            jnp.where(column == index, scale[...], 0.0), axis=1, keepdims=True
        )
        out_ref[0, i] = lagged[: LANES // 2]
        out_ref[1, i] = lagged[LANES // 2 :]


def body(n_chan, n_tm, traces, live_channel, valid_segment):
    forward, inverse, smooth, box = make_tables()
    n = n_chan * n_tm
    n_all = n_chan * CHAN_ROWS
    bins = BINS // n
    piece = min(2, bins)
    pieces = bins // piece
    span = traces.shape[1]
    tables = np.concatenate([*forward, smooth, box], axis=0)
    inverse = np.concatenate(inverse, axis=0)
    vmem = pl.BlockSpec(memory_space=pltpu.VMEM)
    hbm = pl.BlockSpec(memory_space=pltpu.HBM)
    dma = pltpu.SemaphoreType.DMA
    tiles = (ROWS, SUB, LANES)
    crossed = pl.pallas_call(
        functools.partial(spread_kernel, n_chan, n_tm, piece),
        out_shape=jax.ShapeDtypeStruct(tiles, jnp.bfloat16),
        in_specs=[hbm, hbm, vmem, vmem],
        out_specs=hbm,
        scratch_shapes=[
            pltpu.VMEM((CHAN_ROWS, span + 2 * LANES), jnp.float32),
            pltpu.VMEM(tables.shape, jnp.bfloat16),
            pltpu.VMEM((SUB, LANES), jnp.float32),
            pltpu.VMEM((SUB // 2 * ROWS, LANES), jnp.float32),
            pltpu.VMEM(tiles, jnp.bfloat16),
            pltpu.VMEM(tiles, jnp.bfloat16),
            pltpu.VMEM((bins * 2 * n_tm * SEGS, 2 * n_all), jnp.bfloat16),
            pltpu.VMEM((piece, n_all, 2 * n_all), jnp.float32),
            pltpu.VMEM(tiles, jnp.bfloat16),
            dma((2,)), dma((2,)), dma((4 + pieces,)),
            dma((2 * n,)), dma((2 * n,)), dma((pieces * n,)), dma((pieces * n,)),
        ],
        compiler_params=pltpu.CompilerParams(
            collective_id=0, has_side_effects=True, vmem_limit_bytes=40 * 1024 * 1024
        ),
        name="spread",
    )(traces, tables, live_channel.reshape(1, CHAN_ROWS), valid_segment)
    steps = 4
    lagged = pl.pallas_call(
        functools.partial(lag_kernel, steps),
        out_shape=jax.ShapeDtypeStruct((2, SUB, LANES // 2, SEG_LEN), jnp.float32),
        grid=(steps,),
        in_specs=[
            pl.BlockSpec(tiles, lambda i: (0, 0, 0)),
            pl.BlockSpec((2 * ROWS, SEG_LEN), lambda i: (0, 0)),
        ],
        out_specs=pl.BlockSpec((2, SUB // steps, LANES // 2, SEG_LEN), lambda i: (0, i, 0, 0)),
        scratch_shapes=[
            pltpu.VMEM((SUB * ROWS, LANES), jnp.float32),
            pltpu.VMEM((LANES, SUB), jnp.float32),
        ],
        compiler_params=pltpu.CompilerParams(vmem_limit_bytes=32 * 1024 * 1024),
        name="lags",
    )(crossed, inverse)
    return lagged.reshape(CHAN_ROWS, LANES // 2, SEG_LEN)


def solution(mesh):
    n_chan, n_tm = mesh.shape["chan"], mesh.shape["tm"]
    return jax.shard_map(
        functools.partial(body, n_chan, n_tm),
        mesh=mesh,
        in_specs=(P("chan", "tm"), P("chan"), P("chan", "tm")),
        out_specs=P("chan", "tm", None),
        check_vma=False,
    )
```

time: 75.9 us -> 71 us (0.935)
  Pallas kernels: 69.4 us -> 66.7 us
  local copies, waits for them, and re-layouts: 5.42 us -> 4.05 us
  other arithmetic: 0.79 us -> 0 us
    pallas_call x1, Pallas kernels: 64.8 us -> 62.2 us  [body(): pl.pallas_call(functools.partial(spread_kernel, n_chan, n_tm, piece), out...]
    unnamed x14 -> x10, local copies, waits for them, and re-layouts: 5.27 us -> 4.05 us
    transpose x1 -> x0, other arithmetic: 0.79 us -> none  [body(): mask = mask.T.reshape(SUB, LANES)]
where the time goes in v2:
time: 71 us; the launch traced here: 70.7 us
  Pallas kernels  66.7 us (94%)
  local copies, waits for them, and re-layouts  4.05 us (6%)
    pallas_call x1, Pallas kernels, body(): pl.pallas_call(functools.partial(spread_kernel, n_chan, n_tm, piece), out...  62.2 us
    pallas_call x1, Pallas kernels, body(): pl.pallas_call(functools.partial(lag_kernel, steps), out_shape=jax.ShapeD...  4.45 us
    unnamed x10, local copies, waits for them, and re-layouts  4.05 us

profile of v2, /device:TPU:25, one launch (start us, length us, event | category | flops | bytes accessed | tf_op | source)
XLA Modules:
  0.0 70.7 jit_solution(14136850047385020430)
XLA Ops:
  0.0 0.0 copy-start
  0.0 1.6 %copy-done = f32[32,16384]{1,0:T(8,128)S(1)} copy-done((f32[32,16384]{1,0:T(8,128)S(1)}, f32[32,16384]{1,0:T(8,128)}, u32[]{:S(2)}) %copy-start) | copy-done | bytes 2097176
  1.6 0.0 copy-start.1
  1.6 1.1 %copy-done.1 = bf16[1280,256]{1,0:T(8,128)(2,1)S(1)} copy-done((bf16[1280,256]{1,0:T(8,128)(2,1)S(1)}, bf16[1280,256]{1,0:T(8,128)(2,1)}, u32[]{:S(2)}) %copy-start.1) | copy-done | bytes 655384
  2.7 0.0 copy-start.3
  2.7 0.7 %copy-done.3 = s32[32,64]{1,0:T(8,128)S(1)} copy-done((s32[32,64]{1,0:T(8,128)S(1)}, s32[32,64]{1,0:T(8,128)}, u32[]{:S(2)}) %copy-start.3) | copy-done | bytes 8216
  3.4 0.0 copy-start.4
  3.4 0.7 copy-done.4
  4.1 0.0 copy-start.2
  4.1 62.2 %spread.1.cross_ref = bf16[256,16,128]{2,1,0:T(8,128)(2,1)S(1)} custom-call(f32[32,16384]{1,0:T(8,128)S(1)} %copy-done, bf16[1280,256]{1,0:T(8,128)(2,1)S(1)} %copy-done.1, s32[1,32]{1,0:T(1,128)S(1)} %bitcast.2, s32[32,64]{1,0:T(8,128)S(1)} %copy-done.3), custom_call_target="tpu_custom_call" | custom-call | tf_op jit(solution)/shard_map/spread/pallas_call | solution.py:404
  66.3 0.0 copy-done.2
  66.3 4.5 %lags.1 = f32[2,16,64,256]{3,2,1,0:T(8,128)} custom-call(bf16[256,16,128]{2,1,0:T(8,128)(2,1)S(1)} %spread.1.cross_ref, bf16[512,256]{1,0:T(8,128)(2,1)S(1)} %copy-done.2), custom_call_target="tpu_custom_call" | custom-call | tf_op jit(solution)/shard_map/lags/pallas_call | solution.py:428
Async XLA Ops:
  0.0 1.6 %copy-start = (f32[32,16384]{1,0:T(8,128)S(1)}, f32[32,16384]{1,0:T(8,128)}, u32[]{:S(2)}) copy-start(f32[32,16384]{1,0:T(8,128)} %x_hbm.1) | copy-start | bytes 6291460
  1.6 1.1 %copy-start.1 = (bf16[1280,256]{1,0:T(8,128)(2,1)S(1)}, bf16[1280,256]{1,0:T(8,128)(2,1)}, u32[]{:S(2)}) copy-start(bf16[1280,256]{1,0:T(8,128)(2,1)} %constant.4.clone.table_hbm) | copy-start | bytes 1966084
  2.7 0.7 %copy-start.3 = (s32[32,64]{1,0:T(8,128)S(1)}, s32[32,64]{1,0:T(8,128)}, u32[]{:S(2)}) copy-start(s32[32,64]{1,0:T(8,128)} %valid_ref.1) | copy-start | bytes 24580
  3.4 0.7 copy-start.4
  4.1 62.2 %copy-start.2 = (bf16[512,256]{1,0:T(8,128)(2,1)S(1)}, bf16[512,256]{1,0:T(8,128)(2,1)}, u32[]{:S(2)}) copy-start(bf16[512,256]{1,0:T(8,128)(2,1)} %constant.5.clone.inverse_ref) | copy-start | bytes 786436

commit v3 on v2

--- a/solution.py
+++ b/solution.py
@@ -19,6 +19,7 @@
 SEGS = 64
 PER_LANE = LANES // CHAN_ROWS
 MESH = pl.DeviceIdType.MESH
+VMEM_LIMIT = 63 * 1024 * 1024
 
 
 def split_table(table):
@@ -66,8 +67,8 @@
     n_chan, n_tm, piece,
     x_hbm, table_hbm, live_ref, valid_ref,
     out_hbm,
-    xpad, tables, mask_rows, turned, send1, recv1, pair, cross, send2,
-    halo_send, halo_recv, local_sem, send1_sem, recv1_sem, send2_sem, recv2_sem,
+    xpad, tables, mask_rows, turned, send1, recv1, near1, pair, near_pair, cross, near_cross, send2,
+    halo_send, halo_recv, local_sem, send1_sem, recv1_sem, near_send, near_recv, send2_sem, recv2_sem,
 ):
     n = n_chan * n_tm
     span = SEGS * SEG_LEN
@@ -75,6 +76,9 @@
     pieces = bins // piece
     chan, tm = lax.axis_index("chan"), lax.axis_index("tm")
     me = chan * n_tm + tm
+    side = chan // (n_chan // 2)
+    base = side * (n // 2)
+    partner = lax.rem(me + n // 2, n)
 
     def device(index):
         return {"chan": index // n_tm, "tm": lax.rem(index, n_tm)}
@@ -172,46 +176,50 @@
                 :, u * LANES : (u + 1) * LANES
             ]
 
-    def exchange(source, target, size, place, send_sem, recv_sem, sems, local):
-        def copy(part, spot, to, at):
-            return pltpu.make_async_remote_copy(
-                src_ref=source.at[pl.ds(place(part), size)],
-                dst_ref=target.at[pl.ds(place(spot), size)],
-                send_sem=send_sem.at[sems + to], recv_sem=recv_sem.at[sems + at],
-                device_id=device(to), device_id_type=MESH,
-            )
-
-        own = pltpu.make_async_copy(
-            source.at[pl.ds(place(me), size)], target.at[pl.ds(place(me), size)], local
-        )
-
-        def start():
-            def one(k, _):
-                to = lax.rem(me + k, n)
-                copy(to, me, to, me).start()
-                return 0
-
-            lax.fori_loop(1, n, one, 0)
-            own.start()
-
-        def arrive(frm):
-            copy(frm, frm, frm, frm).wait_recv()
-
-        def leave():
-            def one(k, _):
-                to = lax.rem(me + k, n)
-                copy(to, me, to, me).wait_send()
-                return 0
-
-            lax.fori_loop(1, n, one, 0)
-
-        return start, own.wait, arrive, leave
-
-    def spread(h):
-        return exchange(
-            send1, recv1, bins, lambda d: h * BINS + d * bins,
-            send1_sem, recv1_sem, h * n, local_sem.at[2 + h],
-        )
+    def send(source, target, size, place_out, place_in, out_sem, in_sem, to):
+        return pltpu.make_async_remote_copy(
+            src_ref=source.at[pl.ds(place_out, size)], dst_ref=target.at[pl.ds(place_in, size)],
+            send_sem=out_sem, recv_sem=in_sem, device_id=device(to), device_id_type=MESH,
+        )
+
+    def far(h, to, owner):
+        return send(
+            send1, recv1, bins, h * BINS + to * bins, h * BINS + owner * bins,
+            send1_sem.at[h * n + to], recv1_sem.at[h * n + owner], to,
+        )
+
+    def near(h, to, owner):
+        return send(
+            send1, near1, bins, h * BINS + lax.rem(base + to + n // 2, n) * bins,
+            (h * (n // 2) + owner) * bins,
+            near_send.at[h * (n // 2) + to], near_recv.at[h * (n // 2) + owner], base + to,
+        )
+
+    def keep_far(h):
+        return pltpu.make_async_copy(
+            send1.at[pl.ds(h * BINS + me * bins, bins)],
+            recv1.at[pl.ds(h * BINS + me * bins, bins)], local_sem.at[2 + h],
+        )
+
+    def keep_near(h):
+        return pltpu.make_async_copy(
+            send1.at[pl.ds(h * BINS + partner * bins, bins)],
+            near1.at[pl.ds((h * (n // 2) + me - base) * bins, bins)], local_sem.at[4 + h],
+        )
+
+    def each_far(act):
+        def one(k, _):
+            act(lax.rem(me + k, n))
+            return 0
+
+        lax.fori_loop(1, n, one, 0)
+
+    def each_near(act):
+        def one(k, _):
+            act(lax.rem(me - base + k, n // 2))
+            return 0
+
+        lax.fori_loop(1, n // 2, one, 0)
 
     fill.wait()
     load.wait()
@@ -246,7 +254,10 @@
             return 0
 
         lax.fori_loop(0, BINS // 8, turn, 0)
-        spread(h)[0]()
+        each_far(lambda to: far(h, to, me).start())
+        each_near(lambda to: near(h, to, me - base).start())
+        keep_far(h).start()
+        keep_near(h).start()
         return 0
 
     lax.fori_loop(0, 2, half, 0)
@@ -264,96 +275,181 @@
             jnp.where(keep, pltpu.roll(first, LANES - distance, 1), second),
         )
 
+    def arrange(tiles, into, width, at, g):
+        p0, p2 = swap(tiles[0], tiles[2], 64, low_half)
+        p1, p3 = swap(tiles[1], tiles[3], 64, low_half)
+        u0, u1 = swap(p0, p1, 32, even)
+        u2, u3 = swap(p2, p3, 32, even)
+        left = pl.multiple_of(g * LANES, LANES)
+        right = pl.multiple_of(width + g * LANES, LANES)
+        for q, value in enumerate((u0, u1, u2, u3)):
+            rows = pl.ds(pl.multiple_of(at + q * SUB, SUB), SUB)
+            other = jnp.concatenate([value[SUB // 2 :], -value[: SUB // 2]], axis=0)
+            into[rows, pl.ds(left, LANES)] = value.astype(jnp.bfloat16)
+            into[rows, pl.ds(right, LANES)] = other.astype(jnp.bfloat16)
+
     def gather(h, _):
-        _, own_wait, arrive, _ = spread(h)
-        own_wait()
-
-        def group(j, _):
+        keep_far(h).wait()
+        keep_near(h).wait()
+
+        def near_group(j, _):
+            b = lax.rem(j, n_tm)
+            g = j // n_tm
+            sources = [(g * PER_LANE + i) * n_tm + b for i in range(PER_LANE)]
+            for source in sources:
+                @pl.when(source != me - base)
+                def _():
+                    near(h, source, source).wait_recv()
+
+            for f in range(bins):
+                tiles = [
+                    near1[(h * (n // 2) + source) * bins + f].astype(jnp.float32)
+                    for source in sources
+                ]
+                arrange(tiles, near_pair, n_half, f * depth + (h * n_tm + b) * PER_LANE * SUB, g)
+            return 0
+
+        lax.fori_loop(0, n // 2 // PER_LANE, near_group, 0)
+
+        def far_group(j, _):
             b = lax.rem(j, n_tm)
             g = lax.rem(chan // PER_LANE + j // n_tm, groups)
             sources = [(g * PER_LANE + i) * n_tm + b for i in range(PER_LANE)]
             for source in sources:
                 @pl.when(source != me)
                 def _():
-                    arrive(source)
+                    far(h, source, source).wait_recv()
 
             for f in range(bins):
                 tiles = [
                     recv1[h * BINS + source * bins + f].astype(jnp.float32) for source in sources
                 ]
-                p0, p2 = swap(tiles[0], tiles[2], 64, low_half)
-                p1, p3 = swap(tiles[1], tiles[3], 64, low_half)
-                u0, u1 = swap(p0, p1, 32, even)
-                u2, u3 = swap(p2, p3, 32, even)
-                for q, value in enumerate((u0, u1, u2, u3)):
-                    at = pl.multiple_of(
-                        f * depth + ((h * n_tm + b) * PER_LANE + q) * SUB, SUB
-                    )
-                    left = pl.multiple_of(g * LANES, LANES)
-                    right = pl.multiple_of(n_all + g * LANES, LANES)
-                    other = jnp.concatenate([value[SUB // 2 :], -value[: SUB // 2]], axis=0)
-                    pair[pl.ds(at, SUB), pl.ds(left, LANES)] = value.astype(jnp.bfloat16)
-                    pair[pl.ds(at, SUB), pl.ds(right, LANES)] = other.astype(jnp.bfloat16)
-            return 0
-
-        lax.fori_loop(0, n // PER_LANE, group, 0)
+                arrange(tiles, pair, n_all, f * depth + (h * n_tm + b) * PER_LANE * SUB, g)
+            return 0
+
+        lax.fori_loop(0, n // PER_LANE, far_group, 0)
         return 0
 
+    n_half = n_all // 2
     lax.fori_loop(0, 2, gather, 0)
 
-    def back(s):
-        return exchange(
-            send2, out_hbm, 2 * piece, lambda d: (d * bins + s * piece) * 2,
-            send2_sem, recv2_sem, s * n, local_sem.at[4 + s],
+    half_a, half_b = n_chan // 2, n_tm // 2
+    paired = tm // half_b == side
+
+    def back(s, slot, mine):
+        a, b = slot // n_tm, lax.rem(slot, n_tm)
+        spare = jnp.logical_and(a // half_a != side, b // half_b != side)
+        moved = lax.rem(a + half_a, n_chan) * n_tm + lax.rem(b + half_b, n_tm)
+        to = jnp.where(spare, moved, slot)
+        owner = jnp.where(spare, partner, me) if mine else slot
+        return to, send(
+            send2, out_hbm, 2 * piece, (slot * bins + s * piece) * 2,
+            (owner * bins + s * piece) * 2,
+            send2_sem.at[s * n + slot], recv2_sem.at[s * n + owner], to,
+        )
+
+    def keep_back(s):
+        return pltpu.make_async_copy(
+            send2.at[pl.ds((me * bins + s * piece) * 2, 2 * piece)],
+            out_hbm.at[pl.ds((me * bins + s * piece) * 2, 2 * piece)], local_sem.at[6 + 2 * s],
+        )
+
+    def keep_spare(s):
+        slot = lax.rem(chan + half_a, n_chan) * n_tm + lax.rem(tm + half_b, n_tm)
+        return pltpu.make_async_copy(
+            send2.at[pl.ds((slot * bins + s * piece) * 2, 2 * piece)],
+            out_hbm.at[pl.ds((partner * bins + s * piece) * 2, 2 * piece)],
+            local_sem.at[7 + 2 * s],
         )
 
     def some_bins(s, _):
         for i in range(piece):
-            at = pl.multiple_of((s * piece + i) * depth, depth)
-            cross[i] = mm(pair[pl.ds(at, depth), :n_all], pair[pl.ds(at, depth), :], TN)
+            at = pl.ds(pl.multiple_of((s * piece + i) * depth, depth), depth)
+            cross[i] = mm(pair[at, :n_all], pair[at, :], TN)
+            near_cross[i] = mm(near_pair[at, :n_half], near_pair[at, :], TN)
+
+        def pack(block, width, i, row, lane_block, owner, slot_a, slot_b):
+            f = s * piece + i
+            at = pl.multiple_of(row * CHAN_ROWS, CHAN_ROWS)
+            tops = []
+            for c in range(2):
+                lanes = pl.ds(pl.multiple_of(c * width + lane_block * LANES, LANES), LANES)
+                top = block[i, pl.ds(at, SUB), lanes]
+                bottom = block[i, pl.ds(at + SUB, SUB), lanes]
+                tops.append(swap(top, bottom, 64, low_half))
+            for e in range(2):
+                dest = ((slot_a * n_tm + slot_b + e) * bins + f) * 2
+                real = tops[0][e].astype(jnp.bfloat16)
+                imag = tops[1][e]
+                if i == 0:
+                    rest = tops[0][e] - real.astype(jnp.float32)
+                    imag = jnp.where(jnp.logical_and(owner == 0, f == 0), rest, imag)
+                send2[dest] = real
+                send2[dest + 1] = imag.astype(jnp.bfloat16)
+
         for i in range(piece):
-            f = s * piece + i
-            counts = jnp.logical_and(me == 0, f == 0)
-            for a in range(n_chan):
+            for k in range(half_a):
+                mine, others = side * half_a + k, (1 - side) * half_a + k
                 for p in range(n_tm // 2):
-                    tops = []
-                    for c in range(2):
-                        at = c * n_all + p * LANES
-                        top = cross[i, a * CHAN_ROWS : a * CHAN_ROWS + SUB, at : at + LANES]
-                        bottom = cross[
-                            i, a * CHAN_ROWS + SUB : (a + 1) * CHAN_ROWS, at : at + LANES
-                        ]
-                        tops.append(swap(top, bottom, 64, low_half))
-                    for e in range(2):
-                        dest = ((a * n_tm + 2 * p + e) * bins + f) * 2
-                        real = tops[0][e].astype(jnp.bfloat16)
-                        imag = tops[1][e]
-                        if i == 0:
-                            rest = tops[0][e] - real.astype(jnp.float32)
-                            imag = jnp.where(counts, rest, imag)
-                        send2[dest] = real
-                        send2[dest + 1] = imag.astype(jnp.bfloat16)
-        back(s)[0]()
+                    pack(cross, n_all, i, mine, p, me, mine, 2 * p)
+                for p in range(half_b // 2):
+                    inside = side * (half_b // 2) + p
+                    pack(cross, n_all, i, others, inside, me, others, 2 * inside)
+                    pack(
+                        near_cross, n_half, i, k, p, partner, others,
+                        (1 - side) * half_b + 2 * p,
+                    )
+
+        def one(k, _):
+            to, copy = back(s, lax.rem(me + k, n), True)
+
+            @pl.when(to != me)
+            def _():
+                copy.start()
+
+            return 0
+
+        lax.fori_loop(1, n, one, 0)
+        keep_back(s).start()
+
+        @pl.when(paired)
+        def _():
+            keep_spare(s).start()
+
         return 0
 
     lax.fori_loop(0, pieces, some_bins, 0)
 
     def finish(s, _):
-        _, own_wait, arrive, leave = back(s)
-        own_wait()
+        keep_back(s).wait()
+
+        @pl.when(paired)
+        def _():
+            keep_spare(s).wait()
 
         def one(k, _):
-            arrive(lax.rem(me + n - k, n))
+            owner = lax.rem(me + n - k, n)
+
+            @pl.when(jnp.logical_not(jnp.logical_and(paired, owner == partner)))
+            def _():
+                back(s, owner, False)[1].wait_recv()
+
+            to, copy = back(s, lax.rem(me + k, n), True)
+
+            @pl.when(to != me)
+            def _():
+                copy.wait_send()
+
             return 0
 
         lax.fori_loop(1, n, one, 0)
-        leave()
         return 0
 
     lax.fori_loop(0, pieces, finish, 0)
 
     def done(h, _):
-        spread(h)[3]()
+        each_far(lambda to: far(h, to, me).wait_send())
+        each_near(lambda to: near(h, to, me - base).wait_send())
         return 0
 
     lax.fori_loop(0, 2, done, 0)
@@ -413,14 +509,18 @@
             pltpu.VMEM((SUB // 2 * ROWS, LANES), jnp.float32),
             pltpu.VMEM(tiles, jnp.bfloat16),
             pltpu.VMEM(tiles, jnp.bfloat16),
+            pltpu.VMEM((BINS, SUB, LANES), jnp.bfloat16),
             pltpu.VMEM((bins * 2 * n_tm * SEGS, 2 * n_all), jnp.bfloat16),
+            pltpu.VMEM((bins * 2 * n_tm * SEGS, n_all), jnp.bfloat16),
             pltpu.VMEM((piece, n_all, 2 * n_all), jnp.float32),
+            pltpu.VMEM((piece, n_all // 2, n_all), jnp.float32),
             pltpu.VMEM(tiles, jnp.bfloat16),
-            dma((2,)), dma((2,)), dma((4 + pieces,)),
-            dma((2 * n,)), dma((2 * n,)), dma((pieces * n,)), dma((pieces * n,)),
+            dma((2,)), dma((2,)), dma((6 + 2 * pieces,)),
+            dma((2 * n,)), dma((2 * n,)), dma((n,)), dma((n,)),
+            dma((pieces * n,)), dma((pieces * n,)),
         ],
         compiler_params=pltpu.CompilerParams(
-            collective_id=0, has_side_effects=True, vmem_limit_bytes=40 * 1024 * 1024
+            collective_id=0, has_side_effects=True, vmem_limit_bytes=VMEM_LIMIT
         ),
         name="spread",
     )(traces, tables, live_channel.reshape(1, CHAN_ROWS), valid_segment)
@@ -438,7 +538,7 @@
             pltpu.VMEM((SUB * ROWS, LANES), jnp.float32),
             pltpu.VMEM((LANES, SUB), jnp.float32),
         ],
-        compiler_params=pltpu.CompilerParams(vmem_limit_bytes=32 * 1024 * 1024),
+        compiler_params=pltpu.CompilerParams(vmem_limit_bytes=VMEM_LIMIT),
         name="lags",
     )(crossed, inverse)
     return lagged.reshape(CHAN_ROWS, LANES // 2, SEG_LEN)

time: 71 us -> 65 us (0.915)
  the two profiles are of different devices: /device:TPU:25 before, /device:TPU:1 now
where the time goes in v3:
time: 65 us; the launch traced here: 64.7 us
  Pallas kernels  64.7 us (100%)
    pallas_call x1, Pallas kernels, body(): pl.pallas_call(functools.partial(spread_kernel, n_chan, n_tm, piece), out...  59 us
    pallas_call x1, Pallas kernels, body(): pl.pallas_call(functools.partial(lag_kernel, steps), out_shape=jax.ShapeD...  5.7 us

profile of v3, /device:TPU:1, one launch (start us, length us, event | category | flops | bytes accessed | tf_op | source)
XLA Modules:
  0.0 64.7 jit_solution(7931076385538766003)
XLA Ops:
  0.0 59.0 %spread.1.cross_ref = bf16[256,16,128]{2,1,0:T(8,128)(2,1)} custom-call(f32[32,16384]{1,0:T(8,128)} %x_hbm.1, bf16[1280,256]{1,0:T(8,128)(2,1)} %constant.4.clone.table_hbm, s32[1,32]{1,0:T(1,128)} %bitcast.2, s32[32,64]{1,0:T(8,128)} %valid_ref.1), custom_call_target="tpu_custom_call" | custom-call | tf_op jit(solution)/shard_map/spread/pallas_call | solution.py:500
  59.0 5.7 %lags.1 = f32[2,16,64,256]{3,2,1,0:T(8,128)} custom-call(bf16[256,16,128]{2,1,0:T(8,128)(2,1)} %spread.1.cross_ref, bf16[512,256]{1,0:T(8,128)(2,1)} %constant.5.clone.inverse_ref), custom_call_target="tpu_custom_call" | custom-call | tf_op jit(solution)/shard_map/lags/pallas_call | solution.py:528

commit v4 on v3

--- a/solution.py
+++ b/solution.py
@@ -65,9 +65,9 @@
 
 def spread_kernel(
     n_chan, n_tm, piece,
-    x_hbm, table_hbm, live_ref, valid_ref,
+    x_hbm, table_hbm, live_hbm, valid_hbm,
     out_hbm,
-    xpad, tables, mask_rows, turned, send1, recv1, near1, pair, near_pair, cross, near_cross, send2,
+    live_ref, valid_ref, xpad, tables, mask_rows, turned, send1, recv1, near1, pair, near_pair, cross, near_cross, send2,
     halo_send, halo_recv, local_sem, send1_sem, recv1_sem, near_send, near_recv, send2_sem, recv2_sem,
 ):
     n = n_chan * n_tm
@@ -76,13 +76,37 @@
     pieces = bins // piece
     chan, tm = lax.axis_index("chan"), lax.axis_index("tm")
     me = chan * n_tm + tm
-    side = chan // (n_chan // 2)
-    base = side * (n // 2)
-    partner = lax.rem(me + n // 2, n)
-
-    def device(index):
-        return {"chan": index // n_tm, "tm": lax.rem(index, n_tm)}
-
+    half_a, half_b = n_chan // 2, n_tm // 2
+
+    def wrap(index, count):
+        return jnp.where(index >= count, index - count, index)
+
+    def upper(index, half):
+        return (index >= half).astype(jnp.int32)
+
+    side = upper(chan, half_a)
+    near_chan = chan - side * half_a
+    near_me = near_chan * n_tm + tm
+    partner = wrap(chan + half_a, n_chan) * n_tm + tm
+
+    def device(a, b):
+        return {"chan": a, "tm": b}
+
+    def others(first, count, act):
+        for j in range(1, n_tm):
+            act(first, wrap(tm + j, n_tm))
+
+        def one(i, _):
+            for j in range(n_tm):
+                act(wrap(first + i, count), wrap(tm + j, n_tm))
+            return 0
+
+        lax.fori_loop(1, count, one, 0)
+
+    live_in = pltpu.make_async_copy(live_hbm, live_ref, local_sem.at[6])
+    live_in.start()
+    valid_in = pltpu.make_async_copy(valid_hbm, valid_ref, local_sem.at[7])
+    valid_in.start()
     load = pltpu.make_async_copy(table_hbm, tables, local_sem.at[1])
     load.start()
     fill = pltpu.make_async_copy(x_hbm, xpad.at[:, pl.ds(LANES, span)], local_sem.at[0])
@@ -90,13 +114,12 @@
 
     barrier = pltpu.get_barrier_semaphore()
 
-    def greet(k, _):
-        pl.semaphore_signal(
-            barrier, inc=1, device_id=device(lax.rem(me + k, n)), device_id_type=MESH
-        )
-        return 0
-
-    lax.fori_loop(1, n, greet, 0)
+    others(
+        chan, n_chan,
+        lambda a, b: pl.semaphore_signal(
+            barrier, inc=1, device_id=device(a, b), device_id_type=MESH
+        ),
+    )
 
     to_left = pltpu.make_async_remote_copy(
         src_ref=x_hbm.at[:, pl.ds(0, LANES)],
@@ -120,6 +143,8 @@
     def _():
         xpad[:, LANES + span : 2 * LANES + span] = jnp.zeros((CHAN_ROWS, LANES), jnp.float32)
 
+    live_in.wait()
+    valid_in.wait()
     valid = valid_ref[...].astype(jnp.float32).astype(jnp.bfloat16)
     live = live_ref[...].astype(jnp.float32)
     mask_sum = jnp.zeros((SUB, LANES), jnp.float32)
@@ -176,23 +201,23 @@
                 :, u * LANES : (u + 1) * LANES
             ]
 
-    def send(source, target, size, place_out, place_in, out_sem, in_sem, to):
+    def send(source, target, size, place_out, place_in, out_sem, in_sem, a, b):
         return pltpu.make_async_remote_copy(
             src_ref=source.at[pl.ds(place_out, size)], dst_ref=target.at[pl.ds(place_in, size)],
-            send_sem=out_sem, recv_sem=in_sem, device_id=device(to), device_id_type=MESH,
-        )
-
-    def far(h, to, owner):
+            send_sem=out_sem, recv_sem=in_sem, device_id=device(a, b), device_id_type=MESH,
+        )
+
+    def far(h, a, b, owner):
         return send(
-            send1, recv1, bins, h * BINS + to * bins, h * BINS + owner * bins,
-            send1_sem.at[h * n + to], recv1_sem.at[h * n + owner], to,
-        )
-
-    def near(h, to, owner):
+            send1, recv1, bins, h * BINS + (a * n_tm + b) * bins, h * BINS + owner * bins,
+            send1_sem.at[h], recv1_sem.at[h * n + owner], a, b,
+        )
+
+    def near(h, a, b, owner):
         return send(
-            send1, near1, bins, h * BINS + lax.rem(base + to + n // 2, n) * bins,
+            send1, near1, bins, h * BINS + (((1 - side) * half_a + a) * n_tm + b) * bins,
             (h * (n // 2) + owner) * bins,
-            near_send.at[h * (n // 2) + to], near_recv.at[h * (n // 2) + owner], base + to,
+            near_send.at[h], near_recv.at[h * (n // 2) + owner], side * half_a + a, b,
         )
 
     def keep_far(h):
@@ -204,22 +229,8 @@
     def keep_near(h):
         return pltpu.make_async_copy(
             send1.at[pl.ds(h * BINS + partner * bins, bins)],
-            near1.at[pl.ds((h * (n // 2) + me - base) * bins, bins)], local_sem.at[4 + h],
-        )
-
-    def each_far(act):
-        def one(k, _):
-            act(lax.rem(me + k, n))
-            return 0
-
-        lax.fori_loop(1, n, one, 0)
-
-    def each_near(act):
-        def one(k, _):
-            act(lax.rem(me - base + k, n // 2))
-            return 0
-
-        lax.fori_loop(1, n // 2, one, 0)
+            near1.at[pl.ds((h * (n // 2) + near_me) * bins, bins)], local_sem.at[4 + h],
+        )
 
     fill.wait()
     load.wait()
@@ -254,8 +265,8 @@
             return 0
 
         lax.fori_loop(0, BINS // 8, turn, 0)
-        each_far(lambda to: far(h, to, me).start())
-        each_near(lambda to: near(h, to, me - base).start())
+        others(chan, n_chan, lambda a, b: far(h, a, b, me).start())
+        others(near_chan, half_a, lambda a, b: near(h, a, b, near_me).start())
         keep_far(h).start()
         keep_near(h).start()
         return 0
@@ -292,74 +303,75 @@
         keep_far(h).wait()
         keep_near(h).wait()
 
-        def near_group(j, _):
-            b = lax.rem(j, n_tm)
-            g = j // n_tm
-            sources = [(g * PER_LANE + i) * n_tm + b for i in range(PER_LANE)]
-            for source in sources:
-                @pl.when(source != me - base)
-                def _():
-                    near(h, source, source).wait_recv()
-
-            for f in range(bins):
-                tiles = [
-                    near1[(h * (n // 2) + source) * bins + f].astype(jnp.float32)
-                    for source in sources
-                ]
-                arrange(tiles, near_pair, n_half, f * depth + (h * n_tm + b) * PER_LANE * SUB, g)
+        def near_group(g, _):
+            for b in range(n_tm):
+                sources = [(g * PER_LANE + i) * n_tm + b for i in range(PER_LANE)]
+                for i, source in enumerate(sources):
+                    @pl.when(source != near_me)
+                    def _():
+                        near(h, g * PER_LANE + i, b, source).wait_recv()
+
+                for f in range(bins):
+                    tiles = [
+                        near1[(h * (n // 2) + source) * bins + f].astype(jnp.float32)
+                        for source in sources
+                    ]
+                    at = f * depth + (h * n_tm + b) * PER_LANE * SUB
+                    arrange(tiles, near_pair, n_half, at, g)
             return 0
 
-        lax.fori_loop(0, n // 2 // PER_LANE, near_group, 0)
+        lax.fori_loop(0, groups // 2, near_group, 0)
 
         def far_group(j, _):
-            b = lax.rem(j, n_tm)
-            g = lax.rem(chan // PER_LANE + j // n_tm, groups)
-            sources = [(g * PER_LANE + i) * n_tm + b for i in range(PER_LANE)]
-            for source in sources:
-                @pl.when(source != me)
-                def _():
-                    far(h, source, source).wait_recv()
-
-            for f in range(bins):
-                tiles = [
-                    recv1[h * BINS + source * bins + f].astype(jnp.float32) for source in sources
-                ]
-                arrange(tiles, pair, n_all, f * depth + (h * n_tm + b) * PER_LANE * SUB, g)
+            g = wrap(side * (groups // 2) + j, groups)
+            for b in range(n_tm):
+                sources = [(g * PER_LANE + i) * n_tm + b for i in range(PER_LANE)]
+                for i, source in enumerate(sources):
+                    @pl.when(source != me)
+                    def _():
+                        far(h, g * PER_LANE + i, b, source).wait_recv()
+
+                for f in range(bins):
+                    tiles = [
+                        recv1[h * BINS + source * bins + f].astype(jnp.float32)
+                        for source in sources
+                    ]
+                    at = f * depth + (h * n_tm + b) * PER_LANE * SUB
+                    arrange(tiles, pair, n_all, at, g)
             return 0
 
-        lax.fori_loop(0, n // PER_LANE, far_group, 0)
+        lax.fori_loop(0, groups, far_group, 0)
         return 0
 
     n_half = n_all // 2
     lax.fori_loop(0, 2, gather, 0)
 
-    half_a, half_b = n_chan // 2, n_tm // 2
-    paired = tm // half_b == side
-
-    def back(s, slot, mine):
-        a, b = slot // n_tm, lax.rem(slot, n_tm)
-        spare = jnp.logical_and(a // half_a != side, b // half_b != side)
-        moved = lax.rem(a + half_a, n_chan) * n_tm + lax.rem(b + half_b, n_tm)
-        to = jnp.where(spare, moved, slot)
-        owner = jnp.where(spare, partner, me) if mine else slot
-        return to, send(
+    paired = upper(tm, half_b) == side
+    moved_a, moved_b = wrap(chan + half_a, n_chan), wrap(tm + half_b, n_tm)
+
+    def back(s, a, b):
+        slot = a * n_tm + b
+        spare = jnp.logical_and(upper(a, half_a) != side, upper(b, half_b) != side)
+        to_a = jnp.where(spare, wrap(a + half_a, n_chan), a)
+        to_b = jnp.where(spare, wrap(b + half_b, n_tm), b)
+        owner = jnp.where(spare, partner, me)
+        return send(
             send2, out_hbm, 2 * piece, (slot * bins + s * piece) * 2,
-            (owner * bins + s * piece) * 2,
-            send2_sem.at[s * n + slot], recv2_sem.at[s * n + owner], to,
+            (owner * bins + s * piece) * 2, send2_sem.at[0], recv2_sem.at[0], to_a, to_b,
         )
 
     def keep_back(s):
         return pltpu.make_async_copy(
             send2.at[pl.ds((me * bins + s * piece) * 2, 2 * piece)],
-            out_hbm.at[pl.ds((me * bins + s * piece) * 2, 2 * piece)], local_sem.at[6 + 2 * s],
+            out_hbm.at[pl.ds((me * bins + s * piece) * 2, 2 * piece)], local_sem.at[8 + 2 * s],
         )
 
     def keep_spare(s):
-        slot = lax.rem(chan + half_a, n_chan) * n_tm + lax.rem(tm + half_b, n_tm)
+        slot = moved_a * n_tm + moved_b
         return pltpu.make_async_copy(
             send2.at[pl.ds((slot * bins + s * piece) * 2, 2 * piece)],
             out_hbm.at[pl.ds((partner * bins + s * piece) * 2, 2 * piece)],
-            local_sem.at[7 + 2 * s],
+            local_sem.at[9 + 2 * s],
         )
 
     def some_bins(s, _):
@@ -389,27 +401,25 @@
 
         for i in range(piece):
             for k in range(half_a):
-                mine, others = side * half_a + k, (1 - side) * half_a + k
+                mine, outer = side * half_a + k, (1 - side) * half_a + k
                 for p in range(n_tm // 2):
                     pack(cross, n_all, i, mine, p, me, mine, 2 * p)
                 for p in range(half_b // 2):
                     inside = side * (half_b // 2) + p
-                    pack(cross, n_all, i, others, inside, me, others, 2 * inside)
+                    pack(cross, n_all, i, outer, inside, me, outer, 2 * inside)
                     pack(
-                        near_cross, n_half, i, k, p, partner, others,
+                        near_cross, n_half, i, k, p, partner, outer,
                         (1 - side) * half_b + 2 * p,
                     )
 
-        def one(k, _):
-            to, copy = back(s, lax.rem(me + k, n), True)
-
-            @pl.when(to != me)
+        def one(a, b):
+            @pl.when(jnp.logical_not(
+                jnp.logical_and(paired, jnp.logical_and(a == moved_a, b == moved_b))
+            ))
             def _():
-                copy.start()
-
-            return 0
-
-        lax.fori_loop(1, n, one, 0)
+                back(s, a, b).start()
+
+        others(chan, n_chan, one)
         keep_back(s).start()
 
         @pl.when(paired)
@@ -420,39 +430,37 @@
 
     lax.fori_loop(0, pieces, some_bins, 0)
 
-    def finish(s, _):
-        keep_back(s).wait()
+    for p in range(pieces):
+        keep_back(p).wait()
 
         @pl.when(paired)
         def _():
-            keep_spare(s).wait()
-
-        def one(k, _):
-            owner = lax.rem(me + n - k, n)
-
-            @pl.when(jnp.logical_not(jnp.logical_and(paired, owner == partner)))
-            def _():
-                back(s, owner, False)[1].wait_recv()
-
-            to, copy = back(s, lax.rem(me + k, n), True)
-
-            @pl.when(to != me)
-            def _():
-                copy.wait_send()
-
-            return 0
-
-        lax.fori_loop(1, n, one, 0)
-        return 0
-
-    lax.fori_loop(0, pieces, finish, 0)
-
-    def done(h, _):
-        each_far(lambda to: far(h, to, me).wait_send())
-        each_near(lambda to: near(h, to, me - base).wait_send())
-        return 0
-
-    lax.fori_loop(0, 2, done, 0)
+            keep_spare(p).wait()
+
+    def all_back(count):
+        size = count * 2 * bins
+        whole = send(
+            send2, out_hbm, size, 0, 0, send2_sem.at[0], recv2_sem.at[0], moved_a, moved_b
+        )
+        whole.wait_recv()
+        whole.wait_send()
+
+    @pl.when(paired)
+    def _():
+        all_back(n - 2)
+
+    @pl.when(jnp.logical_not(paired))
+    def _():
+        all_back(n - 1)
+
+    for h in range(2):
+        send(
+            send1, recv1, (n - 1) * bins, 0, 0, send1_sem.at[h], recv1_sem.at[0], moved_a, moved_b
+        ).wait_send()
+        send(
+            send1, near1, (n // 2 - 1) * bins, 0, 0, near_send.at[h], near_recv.at[0],
+            moved_a, moved_b,
+        ).wait_send()
 
 
 def lag_kernel(steps, cross_ref, inverse_ref, out_ref, rows, scale):
@@ -493,16 +501,17 @@
     span = traces.shape[1]
     tables = np.concatenate([*forward, smooth, box], axis=0)
     inverse = np.concatenate(inverse, axis=0)
-    vmem = pl.BlockSpec(memory_space=pltpu.VMEM)
     hbm = pl.BlockSpec(memory_space=pltpu.HBM)
     dma = pltpu.SemaphoreType.DMA
     tiles = (ROWS, SUB, LANES)
     crossed = pl.pallas_call(
         functools.partial(spread_kernel, n_chan, n_tm, piece),
         out_shape=jax.ShapeDtypeStruct(tiles, jnp.bfloat16),
-        in_specs=[hbm, hbm, vmem, vmem],
+        in_specs=[hbm] * 4,
         out_specs=hbm,
         scratch_shapes=[
+            pltpu.VMEM((1, CHAN_ROWS), jnp.int32),
+            pltpu.VMEM((CHAN_ROWS, SEGS), jnp.int32),
             pltpu.VMEM((CHAN_ROWS, span + 2 * LANES), jnp.float32),
             pltpu.VMEM(tables.shape, jnp.bfloat16),
             pltpu.VMEM((SUB, LANES), jnp.float32),
@@ -515,9 +524,8 @@
             pltpu.VMEM((piece, n_all, 2 * n_all), jnp.float32),
             pltpu.VMEM((piece, n_all // 2, n_all), jnp.float32),
             pltpu.VMEM(tiles, jnp.bfloat16),
-            dma((2,)), dma((2,)), dma((6 + 2 * pieces,)),
-            dma((2 * n,)), dma((2 * n,)), dma((n,)), dma((n,)),
-            dma((pieces * n,)), dma((pieces * n,)),
+            dma((2,)), dma((2,)), dma((8 + 2 * pieces,)),
+            dma((2,)), dma((2 * n,)), dma((2,)), dma((n,)), dma((1,)), dma((1,)),
         ],
         compiler_params=pltpu.CompilerParams(
             collective_id=0, has_side_effects=True, vmem_limit_bytes=VMEM_LIMIT

time: 65 us -> 61.3 us (0.943)
  Pallas kernels: 64.7 us -> 61.1 us
    pallas_call x1, Pallas kernels: 59 us -> 55.4 us  [body(): pl.pallas_call(functools.partial(spread_kernel, n_chan, n_tm, piece), out...]
where the time goes in v4:
time: 61.3 us; the launch traced here: 61.1 us
  Pallas kernels  61.1 us (100%)
    pallas_call x1, Pallas kernels, body(): pl.pallas_call(functools.partial(spread_kernel, n_chan, n_tm, piece), out...  55.4 us
    pallas_call x1, Pallas kernels, body(): pl.pallas_call(functools.partial(lag_kernel, steps), out_shape=jax.ShapeD...  5.71 us

profile of v4, /device:TPU:1, one launch (start us, length us, event | category | flops | bytes accessed | tf_op | source)
XLA Modules:
  0.0 61.1 jit_solution(2906635442686170030)
XLA Ops:
  0.0 55.4 %spread.1.cross_ref = bf16[256,16,128]{2,1,0:T(8,128)(2,1)} custom-call(f32[32,16384]{1,0:T(8,128)} %x_hbm.1, bf16[1280,256]{1,0:T(8,128)(2,1)} %constant.4.clone.table_hbm, s32[1,32]{1,0:T(1,128)} %bitcast.2, s32[32,64]{1,0:T(8,128)} %valid_hbm.1), custom_call_target="tpu_custom_call" | custom-call | tf_op jit(solution)/shard_map/spread/pallas_call | solution.py:507
  55.4 5.7 %lags.1 = f32[2,16,64,256]{3,2,1,0:T(8,128)} custom-call(bf16[256,16,128]{2,1,0:T(8,128)(2,1)} %spread.1.cross_ref, bf16[512,256]{1,0:T(8,128)(2,1)} %constant.5.clone.inverse_ref), custom_call_target="tpu_custom_call" | custom-call | tf_op jit(solution)/shard_map/lags/pallas_call | solution.py:536

commit v5 on v4

--- a/solution.py
+++ b/solution.py
@@ -14,6 +14,7 @@
 SMOOTH = 4
 ROWS = 2 * BINS
 LANES = 128
+STRIDE = ROWS + 8
 SUB = 16
 CHAN_ROWS = 32
 SEGS = 64
@@ -109,8 +110,17 @@
     valid_in.start()
     load = pltpu.make_async_copy(table_hbm, tables, local_sem.at[1])
     load.start()
-    fill = pltpu.make_async_copy(x_hbm, xpad.at[:, pl.ds(LANES, span)], local_sem.at[0])
-    fill.start()
+    part = 8 * SEG_LEN
+    cuts = (part - LANES, 3 * part + LANES)
+    fills = [
+        pltpu.make_async_copy(
+            x_hbm.at[:, pl.ds(low, high - low)], xpad.at[:, pl.ds(LANES + low, high - low)],
+            local_sem.at[sem],
+        )
+        for sem, low, high in ((0, *cuts), (8 + 2 * pieces, cuts[1], span), (9 + 2 * pieces, 0, cuts[0]))
+    ]
+    for fill in fills:
+        fill.start()
 
     barrier = pltpu.get_barrier_semaphore()
 
@@ -159,16 +169,6 @@
         mask_sum = mask_sum + mm(picked, place)
     mask_rows[...] = mask_sum
 
-    pl.semaphore_wait(barrier, n - 1)
-
-    @pl.when(has_left)
-    def _():
-        to_left.start()
-
-    @pl.when(has_right)
-    def _():
-        to_right.start()
-
     row = lax.broadcasted_iota(jnp.int32, (ROWS, 2 * LANES), 0)
 
     def whiten(m, slot):
@@ -197,9 +197,8 @@
         whitened = spectrum * (mask * lax.rsqrt(smoothed + (0.1 * mean_power + 1e-6)))
         whitened = jnp.where(row == 0, mask, jnp.where(row == 1, 0.0, whitened))
         for u in range(2):
-            turned[pl.ds(pl.multiple_of((2 * slot + u) * ROWS, ROWS), ROWS), :] = whitened[
-                :, u * LANES : (u + 1) * LANES
-            ]
+            at = (2 * slot + u) * STRIDE
+            turned[at : at + ROWS, :] = whitened[:, u * LANES : (u + 1) * LANES]
 
     def send(source, target, size, place_out, place_in, out_sem, in_sem, a, b):
         return pltpu.make_async_remote_copy(
@@ -232,34 +231,47 @@
             near1.at[pl.ds((h * (n // 2) + near_me) * bins, bins)], local_sem.at[4 + h],
         )
 
-    fill.wait()
     load.wait()
+    fills[0].wait()
+    whiten(1, 0)
+    whiten(2, 1)
+    pl.semaphore_wait(barrier, n - 1)
+
+    @pl.when(has_left)
+    def _():
+        to_left.start()
+
+    @pl.when(has_right)
+    def _():
+        to_right.start()
+
+    fills[1].wait()
+    fills[2].wait()
 
     def half(h, _):
-        def two(p, _):
-            @pl.when(jnp.logical_and(h + p == 1, jnp.logical_and(p == 1, has_left)))
+        @pl.when(h == 1)
+        def _():
+            whiten(5, 0)
+            whiten(6, 1)
+
+            @pl.when(has_left)
             def _():
                 to_left.wait_send()
                 to_right.wait_recv()
 
-            @pl.when(jnp.logical_and(h + p == 2, has_right))
+            @pl.when(has_right)
             def _():
                 to_right.wait_send()
                 to_left.wait_recv()
 
-            first = jnp.where(h == 0, 1 + 2 * p, 4 + 2 * p)
-            second = jnp.where(h == 0, 2 - 2 * p, 5 + 2 * p)
-            whiten(first, first - 4 * h)
-            whiten(second, second - 4 * h)
-            return 0
-
-        lax.fori_loop(0, 2, two, 0)
+        whiten(jnp.where(h == 0, 3, 0), 2)
+        whiten(jnp.where(h == 0, 4, 7), 3)
 
         def turn(step, _):
             for i in range(8):
                 f = step * 8 + i
                 tile = jnp.concatenate(
-                    [turned[pl.ds(2 * f + c, SUB // 2, stride=ROWS), :] for c in range(2)], axis=0
+                    [turned[pl.ds(2 * f + c, SUB // 2, stride=STRIDE), :] for c in range(2)], axis=0
                 )
                 send1[h * BINS + f] = tile.astype(jnp.bfloat16)
             return 0
@@ -474,7 +486,7 @@
         def turn(block, _):
             for i in range(16):
                 r = block * 16 + i
-                rows[pl.ds(r, SUB, stride=ROWS), :] = cross_ref[r].astype(jnp.float32)
+                rows[pl.ds(r, SUB, stride=STRIDE), :] = cross_ref[r].astype(jnp.float32)
             return 0
 
         lax.fori_loop(0, ROWS // 16, turn, 0)
@@ -482,7 +494,7 @@
     column = lax.broadcasted_iota(jnp.int32, (LANES, SUB), 1)
     for i in range(SUB // steps):
         index = step * (SUB // steps) + i
-        value = rows[pl.ds(pl.multiple_of(index * ROWS, ROWS), ROWS), :].astype(jnp.bfloat16)
+        value = rows[pl.ds(pl.multiple_of(index * STRIDE, 8), ROWS), :].astype(jnp.bfloat16)
         lagged = mm(value, inverse_ref[:ROWS], TN) + mm(value, inverse_ref[ROWS:], TN)
         lagged = lagged * jnp.sum(
             jnp.where(column == index, scale[...], 0.0), axis=1, keepdims=True
@@ -515,7 +527,7 @@
             pltpu.VMEM((CHAN_ROWS, span + 2 * LANES), jnp.float32),
             pltpu.VMEM(tables.shape, jnp.bfloat16),
             pltpu.VMEM((SUB, LANES), jnp.float32),
-            pltpu.VMEM((SUB // 2 * ROWS, LANES), jnp.float32),
+            pltpu.VMEM((SUB // 2 * STRIDE, LANES), jnp.float32),
             pltpu.VMEM(tiles, jnp.bfloat16),
             pltpu.VMEM(tiles, jnp.bfloat16),
             pltpu.VMEM((BINS, SUB, LANES), jnp.bfloat16),
@@ -524,7 +536,7 @@
             pltpu.VMEM((piece, n_all, 2 * n_all), jnp.float32),
             pltpu.VMEM((piece, n_all // 2, n_all), jnp.float32),
             pltpu.VMEM(tiles, jnp.bfloat16),
-            dma((2,)), dma((2,)), dma((8 + 2 * pieces,)),
+            dma((2,)), dma((2,)), dma((10 + 2 * pieces,)),
             dma((2,)), dma((2 * n,)), dma((2,)), dma((n,)), dma((1,)), dma((1,)),
         ],
         compiler_params=pltpu.CompilerParams(
@@ -543,7 +555,7 @@
         ],
         out_specs=pl.BlockSpec((2, SUB // steps, LANES // 2, SEG_LEN), lambda i: (0, i, 0, 0)),
         scratch_shapes=[
-            pltpu.VMEM((SUB * ROWS, LANES), jnp.float32),
+            pltpu.VMEM((SUB * STRIDE, LANES), jnp.float32),
             pltpu.VMEM((LANES, SUB), jnp.float32),
         ],
         compiler_params=pltpu.CompilerParams(vmem_limit_bytes=VMEM_LIMIT),

time: 61.3 us -> 57.6 us (0.940)
  Pallas kernels: 61.1 us -> 57.4 us
    pallas_call x1, Pallas kernels: 55.4 us -> 53 us  [body(): pl.pallas_call(functools.partial(spread_kernel, n_chan, n_tm, piece), out...]
    pallas_call x1, Pallas kernels: 5.71 us -> 4.44 us  [body(): pl.pallas_call(functools.partial(lag_kernel, steps), out_shape=jax.ShapeD...]
where the time goes in v5:
time: 57.6 us; the launch traced here: 57.4 us
  Pallas kernels  57.4 us (100%)
    pallas_call x1, Pallas kernels, body(): pl.pallas_call(functools.partial(spread_kernel, n_chan, n_tm, piece), out...  53 us
    pallas_call x1, Pallas kernels, body(): pl.pallas_call(functools.partial(lag_kernel, steps), out_shape=jax.ShapeD...  4.44 us

profile of v5, /device:TPU:1, one launch (start us, length us, event | category | flops | bytes accessed | tf_op | source)
XLA Modules:
  0.0 57.4 jit_solution(4437288573284491248)
XLA Ops:
  0.0 53.0 %spread.1.cross_ref = bf16[256,16,128]{2,1,0:T(8,128)(2,1)} custom-call(f32[32,16384]{1,0:T(8,128)} %x_hbm.1, bf16[1280,256]{1,0:T(8,128)(2,1)} %constant.4.clone.table_hbm, s32[1,32]{1,0:T(1,128)} %bitcast.2, s32[32,64]{1,0:T(8,128)} %valid_hbm.1), custom_call_target="tpu_custom_call" | custom-call | tf_op jit(solution)/shard_map/spread/pallas_call | solution.py:519
  53.0 4.4 %lags.1 = f32[2,16,64,256]{3,2,1,0:T(8,128)} custom-call(bf16[256,16,128]{2,1,0:T(8,128)(2,1)} %spread.1.cross_ref, bf16[512,256]{1,0:T(8,128)(2,1)} %constant.5.clone.inverse_ref), custom_call_target="tpu_custom_call" | custom-call | tf_op jit(solution)/shard_map/lags/pallas_call | solution.py:548

commit v6 on v5

--- a/solution.py
+++ b/solution.py
@@ -332,8 +332,6 @@
                     arrange(tiles, near_pair, n_half, at, g)
             return 0
 
-        lax.fori_loop(0, groups // 2, near_group, 0)
-
         def far_group(j, _):
             g = wrap(side * (groups // 2) + j, groups)
             for b in range(n_tm):
@@ -353,6 +351,7 @@
             return 0
 
         lax.fori_loop(0, groups, far_group, 0)
+        lax.fori_loop(0, groups // 2, near_group, 0)
         return 0
 
     n_half = n_all // 2
@@ -508,7 +507,7 @@
     n = n_chan * n_tm
     n_all = n_chan * CHAN_ROWS
     bins = BINS // n
-    piece = min(2, bins)
+    piece = 1
     pieces = bins // piece
     span = traces.shape[1]
     tables = np.concatenate([*forward, smooth, box], axis=0)

time: 57.6 us -> 56.3 us (0.977)
  Pallas kernels: 57.4 us -> 56.2 us
    pallas_call x1, Pallas kernels: 53 us -> 51.7 us  [body(): pl.pallas_call(functools.partial(spread_kernel, n_chan, n_tm, piece), out...]
where the time goes in v6:
time: 56.3 us; the launch traced here: 56.2 us
  Pallas kernels  56.2 us (100%)
    pallas_call x1, Pallas kernels, body(): pl.pallas_call(functools.partial(spread_kernel, n_chan, n_tm, piece), out...  51.7 us
    pallas_call x1, Pallas kernels, body(): pl.pallas_call(functools.partial(lag_kernel, steps), out_shape=jax.ShapeD...  4.44 us

profile of v6, /device:TPU:1, one launch (start us, length us, event | category | flops | bytes accessed | tf_op | source)
XLA Modules:
  0.0 56.2 jit_solution(10289123878430249809)
XLA Ops:
  0.0 51.7 %spread.1.cross_ref = bf16[256,16,128]{2,1,0:T(8,128)(2,1)} custom-call(f32[32,16384]{1,0:T(8,128)} %x_hbm.1, bf16[1280,256]{1,0:T(8,128)(2,1)} %constant.4.clone.table_hbm, s32[1,32]{1,0:T(1,128)} %bitcast.2, s32[32,64]{1,0:T(8,128)} %valid_hbm.1), custom_call_target="tpu_custom_call" | custom-call | tf_op jit(solution)/shard_map/spread/pallas_call | solution.py:518
  51.7 4.4 %lags.1 = f32[2,16,64,256]{3,2,1,0:T(8,128)} custom-call(bf16[256,16,128]{2,1,0:T(8,128)(2,1)} %spread.1.cross_ref, bf16[512,256]{1,0:T(8,128)(2,1)} %constant.5.clone.inverse_ref), custom_call_target="tpu_custom_call" | custom-call | tf_op jit(solution)/shard_map/lags/pallas_call | solution.py:547

commit v7 on v6

--- a/solution.py
+++ b/solution.py
@@ -94,15 +94,16 @@
         return {"chan": a, "tm": b}
 
     def others(first, count, act):
-        for j in range(1, n_tm):
-            act(first, wrap(tm + j, n_tm))
-
-        def one(i, _):
+        def one(t, _):
+            i = t + count // 2 - 1
+            i = jnp.where(i >= count, i - (count - 1), i)
             for j in range(n_tm):
                 act(wrap(first + i, count), wrap(tm + j, n_tm))
             return 0
 
         lax.fori_loop(1, count, one, 0)
+        for j in range(1, n_tm):
+            act(first, wrap(tm + j, n_tm))
 
     live_in = pltpu.make_async_copy(live_hbm, live_ref, local_sem.at[6])
     live_in.start()

time: 56.3 us -> 57.8 us (1.027)
  Pallas kernels: 56.2 us -> 57.3 us
    pallas_call x1, Pallas kernels: 51.7 us -> 52.8 us  [body(): pl.pallas_call(functools.partial(spread_kernel, n_chan, n_tm, piece), out...]
where the time goes in v7:
time: 57.8 us; the launch traced here: 57.3 us
  Pallas kernels  57.3 us (99%)
    pallas_call x1, Pallas kernels, body(): pl.pallas_call(functools.partial(spread_kernel, n_chan, n_tm, piece), out...  52.8 us
    pallas_call x1, Pallas kernels, body(): pl.pallas_call(functools.partial(lag_kernel, steps), out_shape=jax.ShapeD...  4.44 us

profile of v7, /device:TPU:1, one launch (start us, length us, event | category | flops | bytes accessed | tf_op | source)
XLA Modules:
  0.0 57.3 jit_solution(5137689721615794554)
XLA Ops:
  0.0 52.8 %spread.1.cross_ref = bf16[256,16,128]{2,1,0:T(8,128)(2,1)} custom-call(f32[32,16384]{1,0:T(8,128)} %x_hbm.1, bf16[1280,256]{1,0:T(8,128)(2,1)} %constant.4.clone.table_hbm, s32[1,32]{1,0:T(1,128)} %bitcast.2, s32[32,64]{1,0:T(8,128)} %valid_hbm.1), custom_call_target="tpu_custom_call" | custom-call | tf_op jit(solution)/shard_map/spread/pallas_call | solution.py:519
  52.8 4.4 %lags.1 = f32[2,16,64,256]{3,2,1,0:T(8,128)} custom-call(bf16[256,16,128]{2,1,0:T(8,128)(2,1)} %spread.1.cross_ref, bf16[512,256]{1,0:T(8,128)(2,1)} %constant.5.clone.inverse_ref), custom_call_target="tpu_custom_call" | custom-call | tf_op jit(solution)/shard_map/lags/pallas_call | solution.py:548

commit v8 on v6

--- a/solution.py
+++ b/solution.py
@@ -474,11 +474,21 @@
         ).wait_send()
 
 
-def lag_kernel(steps, cross_ref, inverse_ref, out_ref, rows, scale):
+def lag_kernel(steps, cross_hbm, inverse_ref, out_ref, cross_ref, rows, scale, sems):
     step = pl.program_id(0)
 
     @pl.when(step == 0)
     def _():
+        size = ROWS // 4
+        copies = [
+            pltpu.make_async_copy(
+                cross_hbm.at[pl.ds(k * size, size)], cross_ref.at[pl.ds(k * size, size)], sems.at[k]
+            )
+            for k in range(4)
+        ]
+        for copy in copies:
+            copy.start()
+        copies[0].wait()
         count = cross_ref[0].astype(jnp.float32) + cross_ref[1].astype(jnp.float32)
         scale[...] = (2.0 / jnp.maximum(count, 1.0)).T
 
@@ -488,7 +498,10 @@
                 rows[pl.ds(r, SUB, stride=STRIDE), :] = cross_ref[r].astype(jnp.float32)
             return 0
 
-        lax.fori_loop(0, ROWS // 16, turn, 0)
+        for k in range(4):
+            if k > 0:
+                copies[k].wait()
+            lax.fori_loop(k * size // 16, (k + 1) * size // 16, turn, 0)
 
     column = lax.broadcasted_iota(jnp.int32, (LANES, SUB), 1)
     for i in range(SUB // steps):
@@ -549,13 +562,15 @@
         out_shape=jax.ShapeDtypeStruct((2, SUB, LANES // 2, SEG_LEN), jnp.float32),
         grid=(steps,),
         in_specs=[
-            pl.BlockSpec(tiles, lambda i: (0, 0, 0)),
+            hbm,
             pl.BlockSpec((2 * ROWS, SEG_LEN), lambda i: (0, 0)),
         ],
         out_specs=pl.BlockSpec((2, SUB // steps, LANES // 2, SEG_LEN), lambda i: (0, i, 0, 0)),
         scratch_shapes=[
+            pltpu.VMEM(tiles, jnp.bfloat16),
             pltpu.VMEM((SUB * STRIDE, LANES), jnp.float32),
             pltpu.VMEM((LANES, SUB), jnp.float32),
+            dma((4,)),
         ],
         compiler_params=pltpu.CompilerParams(vmem_limit_bytes=VMEM_LIMIT),
         name="lags",

time: 56.3 us -> 57 us (1.012)
  Pallas kernels: 56.2 us -> 56.8 us
    pallas_call x1, Pallas kernels: 4.44 us -> 5.1 us  [body(): pl.pallas_call(functools.partial(lag_kernel, steps), out_shape=jax.ShapeD...]
where the time goes in v8:
time: 57 us; the launch traced here: 56.8 us
  Pallas kernels  56.8 us (100%)
    pallas_call x1, Pallas kernels, body(): pl.pallas_call(functools.partial(spread_kernel, n_chan, n_tm, piece), out...  51.7 us
    pallas_call x1, Pallas kernels, body(): pl.pallas_call(functools.partial(lag_kernel, steps), out_shape=jax.ShapeD...  5.1 us

profile of v8, /device:TPU:1, one launch (start us, length us, event | category | flops | bytes accessed | tf_op | source)
XLA Modules:
  0.0 56.8 jit_solution(13974925652097377772)
XLA Ops:
  0.0 51.7 %spread.1.cross_hbm = bf16[256,16,128]{2,1,0:T(8,128)(2,1)} custom-call(f32[32,16384]{1,0:T(8,128)} %x_hbm.1, bf16[1280,256]{1,0:T(8,128)(2,1)} %constant.4.clone.table_hbm, s32[1,32]{1,0:T(1,128)} %bitcast.2, s32[32,64]{1,0:T(8,128)} %valid_hbm.1), custom_call_target="tpu_custom_call" | custom-call | tf_op jit(solution)/shard_map/spread/pallas_call | solution.py:531
  51.7 5.1 %lags.1 = f32[2,16,64,256]{3,2,1,0:T(8,128)} custom-call(bf16[256,16,128]{2,1,0:T(8,128)(2,1)} %spread.1.cross_hbm, bf16[512,256]{1,0:T(8,128)(2,1)} %constant.5.clone.inverse_ref), custom_call_target="tpu_custom_call" | custom-call | tf_op jit(solution)/shard_map/lags/pallas_call | solution.py:560
